TPU v7x, 256 devices: a whole 4x4x8 slice. The times are simulated.
256 devices in a mesh: grp: 4 (over y_lo, core), blk: 64 (over z, y_hi, x).
Axes of the slice: x: 4, y: 4 (y_hi: 2, y_lo: 2; y = y_hi * 2 + y_lo), z: 8, core: 2. Of those that a mesh axis runs over, the one named last changes fastest.
Arguments:
- images: bfloat16 [131072, 1152], P(('grp', 'blk')), may hold values from -6 to 6
- texts: bfloat16 [131072, 1152], P(('grp', 'blk')), may hold values from -6 to 6
- logit_scale: float32 [1], replicated, may hold values from 30 to 120
- logit_bias: float32 [1], replicated, may hold values from -4 to 0
Outputs:
- image_grad: bfloat16 [131072, 1152], P(('grp', 'blk'))
- text_grad: bfloat16 [131072, 1152], P(('grp', 'blk'))
All inputs are finite; a program needn't handle non-finite values.
Results may differ from a plain program's by a relative error of at most 0.0081.
Values may be sent and summed in bfloat16 or wider, within the bound.
No kernel may reach another device: no remote copies, remote signals or barrier semaphores. Data moves between devices by JAX's collectives and lax.ppermute only.
A program may use at most 64 MiB of HBM per device.

v0:
```python
import jax
import jax.numpy as jnp
from jax import lax
from jax.sharding import PartitionSpec as P


def from_behind(block, axis, distance):
    devices = range(lax.axis_size(axis))
    route = [((i - distance) % len(devices), i) for i in devices]
    return lax.ppermute(block, axis, route)


def partner(block, axis, apart):
    count = lax.axis_size(axis)
    route = []
    for low in range(count):
        high = low | 1 << apart
        if high != low and high < count:
            route += [(low, high), (high, low)]
    return lax.ppermute(block, axis, route)


def unit_rows(raw):
    values = raw.astype(jnp.float32)
    norm = jnp.sqrt(jnp.sum(values * values, axis=-1, keepdims=True) + 1e-06)
    return (values / norm, norm)


def coefficients(left, right, scale, bias, own):
    logits = (
        scale
        * lax.dot_general(left, right, (((1,), (1,)), ((), ())), preferred_element_type=jnp.float32)
        + bias
    )
    count = left.shape[0]
    if own:
        sign = 2.0 * jnp.eye(count, dtype=jnp.float32) - 1.0
    else:
        sign = -jnp.ones((count, count), jnp.float32)
    return (scale * -sign * jax.nn.sigmoid(-sign * logits)).astype(jnp.bfloat16)


def left_product(coef, other):
    return jnp.dot(coef, other, preferred_element_type=jnp.float32)


def right_product(coef, image_rows):
    return lax.dot_general(
        coef, image_rows, (((0,), (0,)), ((), ())), preferred_element_type=jnp.float32
    )


def finish(total, unit, norm):
    return ((total - unit * jnp.sum(unit * total, axis=-1, keepdims=True)) / norm).astype(
        jnp.bfloat16
    )


def on_device(images, texts, logit_scale, logit_bias):
    scale = logit_scale[0]
    bias = logit_bias[0]
    image_unit, image_norm = unit_rows(images)
    text_unit, text_norm = unit_rows(texts)
    image_half = image_unit.astype(jnp.bfloat16)
    text_half = text_unit.astype(jnp.bfloat16)
    text_one = from_behind(text_half, "blk", 1)
    text_two = from_behind(text_half, "blk", 2)
    text_cross = partner(text_half, "grp", 0)
    coef_own = coefficients(image_half, text_half, scale, bias, True)
    coef_one = coefficients(image_half, text_one, scale, bias, False)
    coef_two = coefficients(image_half, text_two, scale, bias, False)
    coef_cross = coefficients(image_half, text_cross, scale, bias, False)
    image_sum = left_product(coef_own, text_half) + left_product(coef_one, text_one)
    image_sum = image_sum + left_product(coef_two, text_two) + left_product(coef_cross, text_cross)
    text_sum = right_product(coef_own, image_half)
    back_one = from_behind(right_product(coef_one, image_half).astype(jnp.bfloat16), "blk", -1)
    back_two = from_behind(right_product(coef_two, image_half).astype(jnp.bfloat16), "blk", -2)
    back_cross = partner(right_product(coef_cross, image_half).astype(jnp.bfloat16), "grp", 0)
    text_sum = (
        text_sum
        + back_one.astype(jnp.float32)
        + back_two.astype(jnp.float32)
        + back_cross.astype(jnp.float32)
    )
    return (finish(image_sum, image_unit, image_norm), finish(text_sum, text_unit, text_norm))


def solution(mesh):
    return jax.shard_map(
        on_device,
        mesh=mesh,
        in_specs=(P(("grp", "blk"), None), P(("grp", "blk"), None), P(), P()),
        out_specs=(P(("grp", "blk"), None), P(("grp", "blk"), None)),
        check_vma=False,
    )
```

profile of v0, /device:TPU:1, one launch (start us, length us, event | category | flops | bytes accessed | tf_op | source)
XLA Modules:
  0.0 145.9 jit_solution(12156477356529380551)
XLA Ops:
  0.6 1.7 %fusion.2 = f32[512]{0:T(512)S(1)} fusion(bf16[512,1152]{1,0:T(8,128)(2,1)} %param.5), kind=kLoop, calls=%fused_computation.11 | loop fusion | flops 1768960 | bytes 1181696 | tf_op jit(solution)/shard_map/reduce_sum | solution.py:25
  2.3 0.0 copy-done
  2.3 0.0 copy-start.1
  2.3 0.4 fusion.33
  2.7 3.3 %collective-permute-start.2 = (bf16[512,1152]{1,0:T(8,128)(2,1)S(1)}, bf16[512,1152]{1,0:T(8,128)(2,1)S(1)}, u32[]{:S(2)}, u32[]{:S(2)}) collective-permute-start(bf16[512,1152]{1,0:T(8,128)(2,1)S(1)} %fusion.33), channel_id=1, source_target_pairs={{0,64},{64,0},{128,192},{192,128},{1,65},{65,1},{129,193},{193,129... | collective-permute-start | bytes 3538952 | tf_op jit(solution)/shard_map/ppermute | solution.py:20
  6.0 0.0 collective-permute-start
  6.0 1.9 %collective-permute-start.1 = (bf16[512,1152]{1,0:T(8,128)(2,1)S(1)}, bf16[512,1152]{1,0:T(8,128)(2,1)S(1)}, u32[]{:S(2)}, u32[]{:S(2)}) collective-permute-start(bf16[512,1152]{1,0:T(8,128)(2,1)S(1)} %fusion.33), channel_id=1, source_target_pairs={{62,0},{63,1},{0,2},{1,3},{2,4},{3,5},{4,6},{5,7},{6,8},{7,9},{8,1... | collective-permute-start | bytes 3538952 | tf_op jit(solution)/shard_map/ppermute | solution.py:10
  8.0 0.3 fusion.1
  9.6 0.4 fusion.32
  10.0 1.1 fusion.28
  11.1 0.9 fusion.34
  11.9 0.0 collective-permute-done.2
  11.9 1.0 fusion.29
  13.0 0.9 convolution_convert_fusion
  13.8 0.7 collective-permute-start.5
  14.6 51.2 %collective-permute-done.1 = bf16[512,1152]{1,0:T(8,128)(2,1)S(1)} collective-permute-done((bf16[512,1152]{1,0:T(8,128)(2,1)S(1)}, bf16[512,1152]{1,0:T(8,128)(2,1)S(1)}, u32[]{:S(2)}, u32[]{:S(2)}) %collective-permute-start.1) | collective-permute-done | bytes 1179680 | tf_op jit(solution)/shard_map/ppermute | solution.py:10
  65.7 1.0 fusion.30
  66.8 0.9 convolution_convert_fusion.1
  67.7 2.1 %collective-permute-start.4 = (bf16[512,1152]{1,0:T(8,128)(2,1)S(1)}, bf16[512,1152]{1,0:T(8,128)(2,1)S(1)}, u32[]{:S(2)}, u32[]{:S(2)}) collective-permute-start(bf16[512,1152]{1,0:T(8,128)(2,1)S(1)} %convolution_convert_fusion.1), channel_id=1, source_target_pairs={{2,0},{3,1},{4,2},{5,3},{6,4},{7,5},{8,6},{9,7},{10,8},{11,9},{12,... | collective-permute-start | bytes 3538952 | tf_op jit(solution)/shard_map/ppermute | solution.py:10
  69.7 0.0 collective-permute-done
  69.7 1.0 fusion.31
  70.8 0.9 convolution_convert_fusion.2
  71.7 18.9 %collective-permute-start.3 = (bf16[512,1152]{1,0:T(8,128)(2,1)S(1)}, bf16[512,1152]{1,0:T(8,128)(2,1)S(1)}, u32[]{:S(2)}, u32[]{:S(2)}) collective-permute-start(bf16[512,1152]{1,0:T(8,128)(2,1)S(1)} %convolution_convert_fusion.2), channel_id=1, source_target_pairs={{1,0},{2,1},{3,2},{4,3},{5,4},{6,5},{7,6},{8,7},{9,8},{10,9},{11,1... | collective-permute-start | bytes 3538952 | tf_op jit(solution)/shard_map/ppermute | solution.py:10
  90.6 0.8 fusion.35
  91.4 0.8 convolution_add_fusion.1
  92.2 1.2 multiply_reduce_fusion.1
  93.4 1.5 %divide_convert_fusion.1 = bf16[512,1152]{1,0:T(8,128)(2,1)} fusion(f32[512,1152]{1,0:T(8,128)S(1)} %get-tuple-element.3, f32[512]{0:T(512)S(1)} %get-tuple-element.2, f32[512]{0:T(512)S(1)} %add_sqrt_fusion.1, bf16[512,1152]{1,0:T(8,128)(2,1)S(1)} %copy-done.1), kind=kLoop, calls=%fused_computation.15 | loop fusion | flops 3538944 | bytes 4722688 | tf_op jit(solution)/shard_map/convert_element_type | solution.py:54
  95.0 0.0 collective-permute-done.5
  95.0 0.6 collective-permute-done.4
  95.5 47.0 %collective-permute-done.3 = bf16[512,1152]{1,0:T(8,128)(2,1)S(1)} collective-permute-done((bf16[512,1152]{1,0:T(8,128)(2,1)S(1)}, bf16[512,1152]{1,0:T(8,128)(2,1)S(1)}, u32[]{:S(2)}, u32[]{:S(2)}) %collective-permute-start.3) | collective-permute-done | bytes 1179680 | tf_op jit(solution)/shard_map/ppermute | solution.py:10
  142.5 1.5 %multiply_reduce_fusion = (f32[512]{0:T(512)S(1)}, f32[512,1152]{1,0:T(8,128)S(1)}) fusion(bf16[512,1152]{1,0:T(8,128)(2,1)S(1)} %collective-permute-done.5, bf16[512,1152]{1,0:T(8,128)(2,1)S(1)} %collective-permute-done.4, bf16[512,1152]{1,0:T(8,128)(2,1)S(1)} %collective-permute-done.3, f32[512]{0:T(512)S(1)} %add_sqrt_fusion, ...), kind=kOutput, calls=%fused_computation.13 | convolution fusion | flops 609877504 | bytes 8785920 | tf_op jit(solution)/shard_map/dot_general | solution.py:48
  144.0 1.9 %divide_convert_fusion = bf16[512,1152]{1,0:T(8,128)(2,1)} fusion(f32[512]{0:T(512)S(1)} %get-tuple-element.4, f32[512]{0:T(512)S(1)} %add_sqrt_fusion, bf16[512,1152]{1,0:T(8,128)(2,1)S(1)} %collective-permute-done.5, bf16[512,1152]{1,0:T(8,128)(2,1)S(1)} %collective-permute-done.4, f32[512,1152]{1,0:T(8,128)S(1)} %get-tuple-element.5, ...), kind=kLoop, calls=%fused_computation.12 | loop fusion | flops 7077888 | bytes 8261632 | tf_op jit(solution)/shard_map/convert_element_type | solution.py:54
  (4 shorter events, 0.0 us)
Async XLA Ops:
  0.6 1.7 %copy-start = (bf16[512,1152]{1,0:T(8,128)(2,1)S(1)}, bf16[512,1152]{1,0:T(8,128)(2,1)}, u32[]{:S(2)}) copy-start(bf16[512,1152]{1,0:T(8,128)(2,1)} %param.5) | copy-start | bytes 3538948
  2.3 5.7 %copy-start.1 = (bf16[512,1152]{1,0:T(8,128)(2,1)S(1)}, bf16[512,1152]{1,0:T(8,128)(2,1)}, u32[]{:S(2)}) copy-start(bf16[512,1152]{1,0:T(8,128)(2,1)} %param.4) | copy-start | bytes 3538948
  2.7 9.2 %collective-permute-start.2 = (bf16[512,1152]{1,0:T(8,128)(2,1)S(1)}, bf16[512,1152]{1,0:T(8,128)(2,1)S(1)}, u32[]{:S(2)}, u32[]{:S(2)}) collective-permute-start(bf16[512,1152]{1,0:T(8,128)(2,1)S(1)} %fusion.33), channel_id=1, source_target_pairs={{0,64},{64,0},{128,192},{192,128},{1,65},{65,1},{129,193},{193,129... | collective-permute-start | bytes 3538952 | tf_op jit(solution)/shard_map/ppermute | solution.py:20
  6.0 63.7 %collective-permute-start = (bf16[512,1152]{1,0:T(8,128)(2,1)S(1)}, bf16[512,1152]{1,0:T(8,128)(2,1)S(1)}, u32[]{:S(2)}, u32[]{:S(2)}) collective-permute-start(bf16[512,1152]{1,0:T(8,128)(2,1)S(1)} %fusion.33), channel_id=1, source_target_pairs={{63,0},{0,1},{1,2},{2,3},{3,4},{4,5},{5,6},{6,7},{7,8},{8,9},{9,10... | collective-permute-start | bytes 3538952 | tf_op jit(solution)/shard_map/ppermute | solution.py:10
  6.0 59.7 %collective-permute-start.1 = (bf16[512,1152]{1,0:T(8,128)(2,1)S(1)}, bf16[512,1152]{1,0:T(8,128)(2,1)S(1)}, u32[]{:S(2)}, u32[]{:S(2)}) collective-permute-start(bf16[512,1152]{1,0:T(8,128)(2,1)S(1)} %fusion.33), channel_id=1, source_target_pairs={{62,0},{63,1},{0,2},{1,3},{2,4},{3,5},{4,6},{5,7},{6,8},{7,9},{8,1... | collective-permute-start | bytes 3538952 | tf_op jit(solution)/shard_map/ppermute | solution.py:10
  13.8 81.1 %collective-permute-start.5 = (bf16[512,1152]{1,0:T(8,128)(2,1)S(1)}, bf16[512,1152]{1,0:T(8,128)(2,1)S(1)}, u32[]{:S(2)}, u32[]{:S(2)}) collective-permute-start(bf16[512,1152]{1,0:T(8,128)(2,1)S(1)} %convolution_convert_fusion), channel_id=1, source_target_pairs={{0,64},{64,0},{128,192},{192,128},{1,65},{65,1},{129,193},{193,129... | collective-permute-start | bytes 3538952 | tf_op jit(solution)/shard_map/ppermute | solution.py:20
  67.7 27.9 %collective-permute-start.4 = (bf16[512,1152]{1,0:T(8,128)(2,1)S(1)}, bf16[512,1152]{1,0:T(8,128)(2,1)S(1)}, u32[]{:S(2)}, u32[]{:S(2)}) collective-permute-start(bf16[512,1152]{1,0:T(8,128)(2,1)S(1)} %convolution_convert_fusion.1), channel_id=1, source_target_pairs={{2,0},{3,1},{4,2},{5,3},{6,4},{7,5},{8,6},{9,7},{10,8},{11,9},{12,... | collective-permute-start | bytes 3538952 | tf_op jit(solution)/shard_map/ppermute | solution.py:10
  71.7 70.8 %collective-permute-start.3 = (bf16[512,1152]{1,0:T(8,128)(2,1)S(1)}, bf16[512,1152]{1,0:T(8,128)(2,1)S(1)}, u32[]{:S(2)}, u32[]{:S(2)}) collective-permute-start(bf16[512,1152]{1,0:T(8,128)(2,1)S(1)} %convolution_convert_fusion.2), channel_id=1, source_target_pairs={{1,0},{2,1},{3,2},{4,3},{5,4},{6,5},{7,6},{8,7},{9,8},{10,9},{11,1... | collective-permute-start | bytes 3538952 | tf_op jit(solution)/shard_map/ppermute | solution.py:10
where the time goes:
time: 146 us
  waiting for transfers between devices  98.7 us (68%)
  starting transfers between devices  27 us (18%)
  matrix products  11.9 us (8%)
  other arithmetic  6.21 us (4%)
  between operations  2.05 us (1%)
    ppermute x4, waiting for transfers between devices, from_behind(): return lax.ppermute(block, axis, route)  98.7 us
    ppermute x4, starting transfers between devices, from_behind(): return lax.ppermute(block, axis, route)  22.9 us
    dot_general x4, matrix products, coefficients(): lax.dot_general(left, right, (((1,), (1,)), ((), ())), preferred_element_...  4.12 us
    dot_general x4, matrix products, right_product(): lax.dot_general(coef, image_rows, (((0,), (0,)), ((), ())), preferred_ele...  4.12 us
    ppermute x2, starting transfers between devices, partner(): return lax.ppermute(block, axis, route)  4.05 us
    dot_general x4, matrix products, left_product(): return jnp.dot(coef, other, preferred_element_type=jnp.float32)  3.71 us
    convert_element_type x2, other arithmetic, finish(): ((total - unit * jnp.sum(unit * total, axis=-1, keepdims=True)) / norm).a...  3.48 us
  transfers between devices with their start and end apart: 6, of which 3 were waited for; matrix products, arithmetic and copies ran while one was open for 9% of the time, Pallas kernels for 0%

commit v1 on v0

v1 whole, which is shorter than its diff:
```python
import jax
import jax.numpy as jnp
from jax import lax
from jax.sharding import PartitionSpec as P

AXES = ("grp", "blk")
CUTS = (0, 256, 512)


def routes(groups, blocks):
    near, far, cross = [], [], []
    for g in range(groups):
        for k in range(blocks):
            me = g * blocks + k
            near.append((me, g * blocks + (k ^ 1)))
            other = (k + 1) % blocks if k % 2 else (k - 1) % blocks
            far.append((me, g * blocks + other))
            cross.append((me, (g ^ 1) * blocks + k))
    return near, far, cross


def unit_rows(raw):
    values = raw.astype(jnp.float32)
    norm = jnp.sqrt(jnp.sum(values * values, axis=-1, keepdims=True) + 1e-06)
    return (values / norm, norm)


def coefficients(left, right, scale, bias, own=False):
    logits = (
        scale
        * lax.dot_general(left, right, (((1,), (1,)), ((), ())), preferred_element_type=jnp.float32)
        + bias
    )
    if own:
        sign = 2.0 * jnp.eye(left.shape[0], dtype=jnp.float32) - 1.0
    else:
        sign = -jnp.ones(logits.shape, jnp.float32)
    return (scale * -sign * jax.nn.sigmoid(-sign * logits)).astype(jnp.bfloat16)


def product(coef, other):
    return jnp.dot(coef, other, preferred_element_type=jnp.float32)


def right_product(coef, rows):
    return lax.dot_general(coef, rows, (((0,), (0,)), ((), ())), preferred_element_type=jnp.float32)


def finish(total, unit, norm):
    return ((total - unit * jnp.sum(unit * total, axis=-1, keepdims=True)) / norm).astype(
        jnp.bfloat16
    )


def on_device(images, texts, logit_scale, logit_bias):
    scale = logit_scale[0]
    bias = logit_bias[0]
    near, far, cross = routes(lax.axis_size("grp"), lax.axis_size("blk"))
    even = lax.axis_index("blk") % 2 == 0
    first = jnp.where(even, texts, images)
    second = jnp.where(even, images, texts)
    first_unit, first_norm = unit_rows(first)
    second_unit, second_norm = unit_rows(second)
    first_half = first_unit.astype(jnp.bfloat16)
    second_half = second_unit.astype(jnp.bfloat16)

    spans = list(zip(CUTS, CUTS[1:]))
    near_in = [lax.ppermute(first_half[a:b], AXES, near) for a, b in spans]
    far_in = [lax.ppermute(second_half[a:b], AXES, far) for a, b in spans]
    near_next = [lax.ppermute(block, AXES, near) for block in far_in]
    far_next = [lax.ppermute(block, AXES, far) for block in near_in]
    first_cross = lax.ppermute(second_half, AXES, cross)
    second_cross = lax.ppermute(first_half, AXES, cross)

    own = coefficients(first_half, second_half, scale, bias, True)
    first_sum = product(own, second_half)
    second_sum = right_product(own, first_half)
    for block in [first_cross] + near_in + near_next:
        first_sum += product(coefficients(first_half, block, scale, bias), block)
    for block in [second_cross] + far_in + far_next:
        second_sum += product(coefficients(second_half, block, scale, bias), block)
    first_grad = finish(first_sum, first_unit, first_norm)
    second_grad = finish(second_sum, second_unit, second_norm)
    return (
        jnp.where(even, second_grad, first_grad),
        jnp.where(even, first_grad, second_grad),
    )


def solution(mesh):
    spec = P(AXES, None)
    return jax.shard_map(
        on_device,
        mesh=mesh,
        in_specs=(spec, spec, P(), P()),
        out_specs=(spec, spec),
        check_vma=False,
    )
```

time: 146 us -> 106 us (0.73)
  the two profiles are of different devices: /device:TPU:1 before, /device:TPU:2 now
where the time goes in v1:
time: 106 us
  matrix products  58 us (55%)
  starting transfers between devices  28 us (26%)
  other arithmetic  8.95 us (8%)
  waiting for transfers between devices  5.72 us (5%)
  local copies, waits for them, and re-layouts  2.83 us (3%)
  between operations  2.02 us (2%)
    dot_general x11, matrix products, product(): return jnp.dot(coef, other, preferred_element_type=jnp.float32)  54.6 us
    ppermute x2, starting transfers between devices, on_device(): near_next = [lax.ppermute(block, AXES, near) for block in far_in]  21.9 us
    ppermute x2, waiting for transfers between devices, on_device(): near_in = [lax.ppermute(first_half[a:b], AXES, near) for a, b in spans]  5.69 us
    select_n x1, other arithmetic, on_device(): jnp.where(even, first_grad, second_grad)  3.85 us
    reduce_sum x1, other arithmetic, unit_rows(): norm = jnp.sqrt(jnp.sum(values * values, axis=-1, keepdims=True) + 1e-06)  2.87 us
    ppermute x2, starting transfers between devices, on_device(): far_in = [lax.ppermute(second_half[a:b], AXES, far) for a, b in spans]  2.49 us
    dot_general x1, matrix products, right_product(): lax.dot_general(coef, rows, (((0,), (0,)), ((), ())), preferred_element_t...  2.32 us
    ppermute x2, starting transfers between devices, on_device(): near_in = [lax.ppermute(first_half[a:b], AXES, near) for a, b in spans]  2.3 us
  transfers between devices with their start and end apart: 10, of which 2 were waited for; matrix products, arithmetic and copies ran while one was open for 50% of the time, Pallas kernels for 0%

profile of v1, /device:TPU:2, one launch (start us, length us, event | category | flops | bytes accessed | tf_op | source)
XLA Modules:
  0.0 105.5 jit_solution(13775666826315334861)
XLA Ops:
  0.7 0.0 copy-start.1
  0.7 2.9 %fusion.5 = (f32[512]{0:T(512)S(1)}, f32[512]{0:T(512)S(1)}) fusion(bf16[512,1152]{1,0:T(8,128)(2,1)} %param.4, bf16[512,1152]{1,0:T(8,128)(2,1)} %param.5, pred[]{:T(512)S(6)} %eq.10), kind=kLoop, calls=%fused_computation.15 | loop fusion | flops 4717568 | bytes 2363393 | tf_op jit(solution)/shard_map/reduce_sum | solution.py:24
  3.6 1.0 fusion.128
  4.6 0.1 collective-permute-start.7
  4.7 0.5 collective-permute-start
  5.2 0.9 fusion.131
  6.1 2.3 %collective-permute-start.5 = (bf16[256,1152]{1,0:T(8,128)(2,1)S(1)}, bf16[256,1152]{1,0:T(8,128)(2,1)S(1)}, u32[]{:S(2)}, u32[]{:S(2)}) collective-permute-start(bf16[256,1152]{1,0:T(8,128)(2,1)S(1)} %get-tuple-element.14), channel_id=1, source_target_pairs={{0,1},{1,0},{2,3},{3,2},{4,5},{5,4},{6,7},{7,6},{8,9},{9,8},{10,11... | collective-permute-start | bytes 1769480 | tf_op jit(solution)/shard_map/ppermute | solution.py:68
  8.4 0.0 collective-permute-start.3
  8.4 1.1 %fusion.130 = (bf16[256,1152]{1,0:T(8,128)(2,1)}, bf16[256,1152]{1,0:T(8,128)(2,1)}) fusion(bf16[512,1152]{1,0:T(8,128)(2,1)S(1)} %get-tuple-element.10), kind=kLoop, calls=%fused_computation.162 | loop fusion | bytes 2359296 | tf_op jit(solution)/shard_map/slice | solution.py:69
  9.5 1.2 %collective-permute-start.2 = (bf16[256,1152]{1,0:T(8,128)(2,1)}, bf16[256,1152]{1,0:T(8,128)(2,1)}, u32[]{:S(2)}, u32[]{:S(2)}) collective-permute-start(bf16[256,1152]{1,0:T(8,128)(2,1)} %get-tuple-element.12), channel_id=1, source_target_pairs={{0,63},{1,2},{2,1},{3,4},{4,3},{5,6},{6,5},{7,8},{8,7},{9,10},{10,... | collective-permute-start | bytes 1769480 | tf_op jit(solution)/shard_map/ppermute | solution.py:69
  12.0 1.1 %fusion.25 = bf16[512,512]{1,0:T(8,128)(2,1)S(1)} fusion(bf16[512,1152]{1,0:T(8,128)(2,1)S(1)} %get-tuple-element.9, bf16[512,1152]{1,0:T(8,128)(2,1)S(1)} %get-tuple-element.10, f32[]{:T(128)} %bitcast.49, f32[]{:T(128)} %bitcast.41), kind=kOutput, calls=%fused_computation.42 | convolution fusion | flops 607387648 | bytes 2883592 | tf_op jit(solution)/shard_map/dot_general | solution.py:31
  13.1 2.3 %fusion.133 = f32[512,1152]{1,0:T(8,128)} fusion(bf16[512,512]{1,0:T(8,128)(2,1)S(1)} %fusion.25, bf16[512,1152]{1,0:T(8,128)(2,1)S(1)} %get-tuple-element.10), kind=kOutput, calls=%fused_computation.165 | convolution fusion | flops 603979776 | bytes 4063232 | tf_op jit(solution)/shard_map/dot_general | solution.py:42
  15.4 2.3 %fusion.132 = f32[512,1152]{1,0:T(8,128)} fusion(bf16[512,512]{1,0:T(8,128)(2,1)S(1)} %fusion.25, bf16[512,1152]{1,0:T(8,128)(2,1)S(1)} %get-tuple-element.9), kind=kOutput, calls=%fused_computation.164 | convolution fusion | flops 603979776 | bytes 4063232 | tf_op jit(solution)/shard_map/dot_general | solution.py:46
  17.8 4.8 %collective-permute-done.5 = bf16[256,1152]{1,0:T(8,128)(2,1)S(1)} collective-permute-done((bf16[256,1152]{1,0:T(8,128)(2,1)S(1)}, bf16[256,1152]{1,0:T(8,128)(2,1)S(1)}, u32[]{:S(2)}, u32[]{:S(2)}) %collective-permute-start.5) | collective-permute-done | bytes 589856 | tf_op jit(solution)/shard_map/ppermute | solution.py:68
  22.5 0.8 copy-done.3
  23.3 1.3 %collective-permute-start.1 = (bf16[256,1152]{1,0:T(8,128)(2,1)}, bf16[256,1152]{1,0:T(8,128)(2,1)}, u32[]{:S(2)}, u32[]{:S(2)}) collective-permute-start(bf16[256,1152]{1,0:T(8,128)(2,1)} %get-tuple-element.11), channel_id=1, source_target_pairs={{0,63},{1,2},{2,1},{3,4},{4,3},{5,6},{6,5},{7,8},{8,7},{9,10},{10,... | collective-permute-start | bytes 1769480 | tf_op jit(solution)/shard_map/ppermute | solution.py:69
  24.6 4.2 %fusion.86 = f32[512,1152]{1,0:T(8,128)} fusion(bf16[256,1152]{1,0:T(8,128)(2,1)} %copy-done.3, bf16[512,1152]{1,0:T(8,128)(2,1)S(1)} %get-tuple-element.9, f32[]{:T(128)} %bitcast.55, f32[]{:T(128)} %bitcast.47), kind=kOutput, calls=%fused_computation.115 | convolution fusion | flops 604897280 | bytes 4128776 | tf_op jit(solution)/shard_map/dot_general | solution.py:42
  28.8 0.7 collective-permute-start.6
  29.6 4.2 %fusion.84 = f32[512,1152]{1,0:T(8,128)} fusion(bf16[256,1152]{1,0:T(8,128)(2,1)} %collective-permute-done.2, bf16[512,1152]{1,0:T(8,128)(2,1)S(1)} %get-tuple-element.10, f32[]{:T(128)} %bitcast.59, f32[]{:T(128)} %bitcast.46), kind=kOutput, calls=%fused_computation.113 | convolution fusion | flops 604897280 | bytes 4128776 | tf_op jit(solution)/shard_map/dot_general | solution.py:42
  33.8 0.9 collective-permute-done.3
  34.7 10.7 %collective-permute-start.9 = (bf16[256,1152]{1,0:T(8,128)(2,1)}, bf16[256,1152]{1,0:T(8,128)(2,1)}, u32[]{:S(2)}, u32[]{:S(2)}) collective-permute-start(bf16[256,1152]{1,0:T(8,128)(2,1)} %collective-permute-done.2), channel_id=1, source_target_pairs={{0,1},{1,0},{2,3},{3,2},{4,5},{5,4},{6,7},{7,6},{8,9},{9,8},{10,11... | collective-permute-start | bytes 1769480 | tf_op jit(solution)/shard_map/ppermute | solution.py:70
  45.5 11.2 %collective-permute-start.8 = (bf16[256,1152]{1,0:T(8,128)(2,1)}, bf16[256,1152]{1,0:T(8,128)(2,1)}, u32[]{:S(2)}, u32[]{:S(2)}) collective-permute-start(bf16[256,1152]{1,0:T(8,128)(2,1)} %collective-permute-done.1), channel_id=1, source_target_pairs={{0,1},{1,0},{2,3},{3,2},{4,5},{5,4},{6,7},{7,6},{8,9},{9,8},{10,11... | collective-permute-start | bytes 1769480 | tf_op jit(solution)/shard_map/ppermute | solution.py:70
  56.6 5.6 %convolution_add_fusion.2 = f32[512,1152]{1,0:T(8,128)} fusion(f32[512,1152]{1,0:T(8,128)} %fusion.133, bf16[512,1152]{1,0:T(8,128)(2,1)} %collective-permute-done.7, bf16[512,1152]{1,0:T(8,128)(2,1)S(1)} %get-tuple-element.9, f32[]{:T(128)} %bitcast.51, f32[]{:T(128)} %bitcast.40), kind=kOutput, calls=%fused_computation.4 | convolution fusion | flops 1210384384 | bytes 7077896 | tf_op jit(solution)/shard_map/dot_general | solution.py:42
  62.2 5.5 %convolution_add_fusion.5 = f32[512,1152]{1,0:T(8,128)} fusion(f32[512,1152]{1,0:T(8,128)} %fusion.132, bf16[512,1152]{1,0:T(8,128)(2,1)} %collective-permute-done, bf16[512,1152]{1,0:T(8,128)(2,1)S(1)} %get-tuple-element.10, f32[]{:T(128)} %bitcast.52, f32[]{:T(128)} %bitcast.38), kind=kOutput, calls=%fused_computation.9 | convolution fusion | flops 1210384384 | bytes 7077896 | tf_op jit(solution)/shard_map/dot_general | solution.py:42
  67.7 5.7 %fusion.1 = f32[512,1152]{1,0:T(8,128)} fusion(f32[512,1152]{1,0:T(8,128)} %fusion.86, f32[512,1152]{1,0:T(8,128)} %convolution_add_fusion.2, bf16[256,1152]{1,0:T(8,128)(2,1)} %collective-permute-done.3, bf16[512,1152]{1,0:T(8,128)(2,1)S(1)} %get-tuple-element.9, f32[]{:T(128)} %bitcast.56, f32[]{:T(128)} %bitcast.43), kind=kOutput, calls=%fused_computation.3 | convolution fusion | flops 606076928 | bytes 8847368 | tf_op jit(solution)/shard_map/dot_general | solution.py:42
  73.4 5.7 %fusion.3 = f32[512,1152]{1,0:T(8,128)} fusion(f32[512,1152]{1,0:T(8,128)} %fusion.84, f32[512,1152]{1,0:T(8,128)} %convolution_add_fusion.5, bf16[256,1152]{1,0:T(8,128)(2,1)} %collective-permute-done.1, bf16[512,1152]{1,0:T(8,128)(2,1)S(1)} %get-tuple-element.10, f32[]{:T(128)} %bitcast.50, f32[]{:T(128)} %bitcast.48), kind=kOutput, calls=%fused_computation.8 | convolution fusion | flops 606076928 | bytes 8847368 | tf_op jit(solution)/shard_map/dot_general | solution.py:42
  79.2 4.3 %fusion.85 = f32[512,1152]{1,0:T(8,128)} fusion(bf16[256,1152]{1,0:T(8,128)(2,1)} %collective-permute-done.6, bf16[512,1152]{1,0:T(8,128)(2,1)S(1)} %get-tuple-element.10, f32[]{:T(128)} %bitcast.57, f32[]{:T(128)} %bitcast.42), kind=kOutput, calls=%fused_computation.114 | convolution fusion | flops 604897280 | bytes 4128776 | tf_op jit(solution)/shard_map/dot_general | solution.py:42
  83.4 4.2 %fusion.87 = f32[512,1152]{1,0:T(8,128)} fusion(bf16[256,1152]{1,0:T(8,128)(2,1)} %collective-permute-done.9, bf16[512,1152]{1,0:T(8,128)(2,1)S(1)} %get-tuple-element.9, f32[]{:T(128)} %bitcast.53, f32[]{:T(128)} %bitcast.39), kind=kOutput, calls=%fused_computation.116 | convolution fusion | flops 604897280 | bytes 4128776 | tf_op jit(solution)/shard_map/dot_general | solution.py:42
  87.6 5.8 %fusion.2 = f32[512,1152]{1,0:T(8,128)} fusion(f32[512,1152]{1,0:T(8,128)} %fusion.85, f32[512,1152]{1,0:T(8,128)} %fusion.3, bf16[256,1152]{1,0:T(8,128)(2,1)} %collective-permute-done.4, bf16[512,1152]{1,0:T(8,128)(2,1)S(1)} %get-tuple-element.10, f32[]{:T(128)} %bitcast.58, f32[]{:T(128)} %bitcast.44), kind=kOutput, calls=%fused_computation.6 | convolution fusion | flops 606076928 | bytes 8847368 | tf_op jit(solution)/shard_map/dot_general | solution.py:42
  93.4 7.1 %multiply_reduce_fusion = (f32[512]{0:T(512)S(1)}, f32[512]{0:T(512)S(1)}, f32[512,1152]{1,0:T(8,128)}) fusion(f32[512]{0:T(512)S(1)} %get-tuple-element.17, bf16[512,1152]{1,0:T(8,128)(2,1)} %param.5, bf16[512,1152]{1,0:T(8,128)(2,1)S(1)} %copy-done, pred[]{:T(512)S(6)} %eq.10, f32[512,1152]{1,0:T(8,128)} %fusion.2, f32[512]{0:T(512)S(1)} %get-tuple-element.16, ...), kind=kOutput, calls=%fused_computation.17 | convolution fusion | flops 611974144 | bytes 13574153 | tf_op jit(solution)/shard_map/dot_general | solution.py:42
  100.5 3.9 %broadcast_select_fusion = (bf16[512,1152]{1,0:T(8,128)(2,1)}, bf16[512,1152]{1,0:T(8,128)(2,1)S(1)}, bf16[512,1152]{1,0:T(8,128)(2,1)S(1)}) fusion(pred[]{:T(512)S(6)} %eq.10, f32[512,1152]{1,0:T(8,128)} %get-tuple-element.15, f32[512]{0:T(512)S(1)} %get-tuple-element.2, f32[512]{0:T(512)S(1)} %get-tuple-element.17, bf16[512,1152]{1,0:T(8,128)(2,1)S(1)} %copy-done.2, ...), kind=kLoop, calls=%fused_computation.109 | loop fusion | flops 8847360 | bytes 10625025 | tf_op jit(solution)/shard_map/jit(_where)/select_n | solution.py:86
  104.4 1.2 %broadcast_select_fusion.1 = bf16[512,1152]{1,0:T(8,128)(2,1)} fusion(bf16[512,1152]{1,0:T(8,128)(2,1)S(1)} %get-tuple-element.8, bf16[512,1152]{1,0:T(8,128)(2,1)S(1)} %get-tuple-element.7, pred[]{:T(512)S(6)} %eq.10), kind=kLoop, calls=%fused_computation.110 | loop fusion | flops 589824 | bytes 3538945 | tf_op jit(solution)/shard_map/jit(_where)/select_n | solution.py:85
  (16 shorter events, 0.0 us)
Async XLA Ops:
  0.6 2.9 %copy-start = (bf16[512,1152]{1,0:T(8,128)(2,1)S(1)}, bf16[512,1152]{1,0:T(8,128)(2,1)}, u32[]{:S(2)}) copy-start(bf16[512,1152]{1,0:T(8,128)(2,1)} %param.4) | copy-start | bytes 3538948
  0.7 2.9 %copy-start.1 = (bf16[512,1152]{1,0:T(8,128)(2,1)S(1)}, bf16[512,1152]{1,0:T(8,128)(2,1)}, u32[]{:S(2)}) copy-start(bf16[512,1152]{1,0:T(8,128)(2,1)} %param.5) | copy-start | bytes 3538948
  4.6 40.9 %collective-permute-start.7 = (bf16[512,1152]{1,0:T(8,128)(2,1)S(1)}, bf16[512,1152]{1,0:T(8,128)(2,1)}, u32[]{:S(2)}, u32[]{:S(2)}) collective-permute-start(bf16[512,1152]{1,0:T(8,128)(2,1)S(1)} %get-tuple-element.10), channel_id=1, source_target_pairs={{0,64},{1,65},{2,66},{3,67},{4,68},{5,69},{6,70},{7,71},{8,72},{9,... | collective-permute-start | bytes 3538952 | tf_op jit(solution)/shard_map/ppermute | solution.py:72
  4.7 57.5 %collective-permute-start = (bf16[512,1152]{1,0:T(8,128)(2,1)S(1)}, bf16[512,1152]{1,0:T(8,128)(2,1)}, u32[]{:S(2)}, u32[]{:S(2)}) collective-permute-start(bf16[512,1152]{1,0:T(8,128)(2,1)S(1)} %get-tuple-element.9), channel_id=1, source_target_pairs={{0,64},{1,65},{2,66},{3,67},{4,68},{5,69},{6,70},{7,71},{8,72},{9,... | collective-permute-start | bytes 3538952 | tf_op jit(solution)/shard_map/ppermute | solution.py:73
  6.1 16.4 %collective-permute-start.5 = (bf16[256,1152]{1,0:T(8,128)(2,1)S(1)}, bf16[256,1152]{1,0:T(8,128)(2,1)S(1)}, u32[]{:S(2)}, u32[]{:S(2)}) collective-permute-start(bf16[256,1152]{1,0:T(8,128)(2,1)S(1)} %get-tuple-element.14), channel_id=1, source_target_pairs={{0,1},{1,0},{2,3},{3,2},{4,5},{5,4},{6,7},{7,6},{8,9},{9,8},{10,11... | collective-permute-start | bytes 1769480 | tf_op jit(solution)/shard_map/ppermute | solution.py:68
  8.4 26.3 %collective-permute-start.3 = (bf16[256,1152]{1,0:T(8,128)(2,1)}, bf16[256,1152]{1,0:T(8,128)(2,1)}, u32[]{:S(2)}, u32[]{:S(2)}) collective-permute-start(bf16[256,1152]{1,0:T(8,128)(2,1)} %get-tuple-element.13), channel_id=1, source_target_pairs={{0,1},{1,0},{2,3},{3,2},{4,5},{5,4},{6,7},{7,6},{8,9},{9,8},{10,11... | collective-permute-start | bytes 1769480 | tf_op jit(solution)/shard_map/ppermute | solution.py:68
  9.5 19.3 %collective-permute-start.2 = (bf16[256,1152]{1,0:T(8,128)(2,1)}, bf16[256,1152]{1,0:T(8,128)(2,1)}, u32[]{:S(2)}, u32[]{:S(2)}) collective-permute-start(bf16[256,1152]{1,0:T(8,128)(2,1)} %get-tuple-element.12), channel_id=1, source_target_pairs={{0,63},{1,2},{2,1},{3,4},{4,3},{5,6},{6,5},{7,8},{8,7},{9,10},{10,... | collective-permute-start | bytes 1769480 | tf_op jit(solution)/shard_map/ppermute | solution.py:69
  22.5 0.8 copy-start.3
  23.3 22.1 %collective-permute-start.1 = (bf16[256,1152]{1,0:T(8,128)(2,1)}, bf16[256,1152]{1,0:T(8,128)(2,1)}, u32[]{:S(2)}, u32[]{:S(2)}) collective-permute-start(bf16[256,1152]{1,0:T(8,128)(2,1)} %get-tuple-element.11), channel_id=1, source_target_pairs={{0,63},{1,2},{2,1},{3,4},{4,3},{5,6},{6,5},{7,8},{8,7},{9,10},{10,... | collective-permute-start | bytes 1769480 | tf_op jit(solution)/shard_map/ppermute | solution.py:69
  28.8 50.3 %collective-permute-start.6 = (bf16[256,1152]{1,0:T(8,128)(2,1)}, bf16[256,1152]{1,0:T(8,128)(2,1)}, u32[]{:S(2)}, u32[]{:S(2)}) collective-permute-start(bf16[256,1152]{1,0:T(8,128)(2,1)} %copy-done.3), channel_id=1, source_target_pairs={{0,63},{1,2},{2,1},{3,4},{4,3},{5,6},{6,5},{7,8},{8,7},{9,10},{10,... | collective-permute-start | bytes 1769480 | tf_op jit(solution)/shard_map/ppermute | solution.py:71
  34.7 48.7 %collective-permute-start.9 = (bf16[256,1152]{1,0:T(8,128)(2,1)}, bf16[256,1152]{1,0:T(8,128)(2,1)}, u32[]{:S(2)}, u32[]{:S(2)}) collective-permute-start(bf16[256,1152]{1,0:T(8,128)(2,1)} %collective-permute-done.2), channel_id=1, source_target_pairs={{0,1},{1,0},{2,3},{3,2},{4,5},{5,4},{6,7},{7,6},{8,9},{9,8},{10,11... | collective-permute-start | bytes 1769480 | tf_op jit(solution)/shard_map/ppermute | solution.py:70
  45.5 42.2 %collective-permute-start.4 = (bf16[256,1152]{1,0:T(8,128)(2,1)}, bf16[256,1152]{1,0:T(8,128)(2,1)}, u32[]{:S(2)}, u32[]{:S(2)}) collective-permute-start(bf16[256,1152]{1,0:T(8,128)(2,1)} %collective-permute-done.3), channel_id=1, source_target_pairs={{0,63},{1,2},{2,1},{3,4},{4,3},{5,6},{6,5},{7,8},{8,7},{9,10},{10,... | collective-permute-start | bytes 1769480 | tf_op jit(solution)/shard_map/ppermute | solution.py:71
  45.5 47.9 %collective-permute-start.8 = (bf16[256,1152]{1,0:T(8,128)(2,1)}, bf16[256,1152]{1,0:T(8,128)(2,1)}, u32[]{:S(2)}, u32[]{:S(2)}) collective-permute-start(bf16[256,1152]{1,0:T(8,128)(2,1)} %collective-permute-done.1), channel_id=1, source_target_pairs={{0,1},{1,0},{2,3},{3,2},{4,5},{5,4},{6,7},{7,6},{8,9},{9,8},{10,11... | collective-permute-start | bytes 1769480 | tf_op jit(solution)/shard_map/ppermute | solution.py:70
  93.4 7.1 %copy-start.2 = (bf16[512,1152]{1,0:T(8,128)(2,1)S(1)}, bf16[512,1152]{1,0:T(8,128)(2,1)}, u32[]{:S(2)}) copy-start(bf16[512,1152]{1,0:T(8,128)(2,1)} %param.5) | copy-start | bytes 3538948

commit v2 on v1

v2 whole, which is shorter than its diff:
```python
import functools

import jax
import jax.numpy as jnp
from jax import lax
from jax.experimental import pallas as pl
from jax.experimental.pallas import tpu as pltpu
from jax.sharding import PartitionSpec as P

AXES = ("grp", "blk")
VMEM = pl.BlockSpec(memory_space=pltpu.VMEM)
SMEM = pl.BlockSpec(memory_space=pltpu.SMEM)
HBM = pl.BlockSpec(memory_space=pltpu.HBM)
TILE = 128
MIB = 1024 * 1024


def routes(groups, blocks):
    near, far, cross = [], [], []
    for g in range(groups):
        for k in range(blocks):
            me = g * blocks + k
            near.append((me, g * blocks + (k ^ 1)))
            other = (k + 1) % blocks if k % 2 else (k - 1) % blocks
            far.append((me, g * blocks + other))
            cross.append((me, (g ^ 1) * blocks + k))
    return near, far, cross


def call(body, outs, in_specs, out_specs, scratch=(), aliases=None, limit=16):
    return pl.pallas_call(
        body,
        out_shape=outs,
        in_specs=in_specs,
        out_specs=out_specs,
        scratch_shapes=scratch,
        input_output_aliases=aliases or {},
        compiler_params=pltpu.CompilerParams(vmem_limit_bytes=limit * MIB),
        cost_estimate=pl.CostEstimate(flops=0, bytes_accessed=0, transcendentals=0),
    )


def shape(rows, width, dtype):
    return jax.ShapeDtypeStruct((rows, width), dtype)


def prepare_kernel(start, even, images, texts, *refs):
    *outs, both, sems = refs
    blocks = (outs[:3], outs[3:])
    rows = blocks[0][0].shape[0]
    tiles = rows // TILE

    def fetch(slot, source, tile):
        return pltpu.make_async_copy(
            source.at[pl.ds(start + tile * TILE, TILE)],
            blocks[slot][1].at[pl.ds(tile * TILE, TILE)],
            sems.at[slot, tile],
        )

    def begin(sources):
        for tile in range(tiles):
            for slot, source in enumerate(sources):
                fetch(slot, source, tile).start()

    @pl.when(even[0] == 1)
    def _():
        begin((texts, images))

    @pl.when(even[0] != 1)
    def _():
        begin((images, texts))

    for tile in range(tiles):
        at = pl.ds(tile * TILE, TILE)
        for slot, (half, raw, norm) in enumerate(blocks):
            fetch(slot, images, tile).wait()
            values = raw[at].astype(jnp.float32)
            size = jnp.sqrt(jnp.sum(values * values, axis=-1, keepdims=True) + 1e-06)
            inverse = 1.0 / size
            rounded = (values * inverse).astype(jnp.bfloat16)
            half[at] = rounded
            both[pl.ds(slot * rows + tile * TILE, TILE)] = rounded
            norm[at] = jnp.broadcast_to(inverse, (TILE, 128))


def prepare(start, rows, even, images, texts):
    width = images.shape[1]
    rounded = shape(rows, width, jnp.bfloat16)
    outs = [rounded, rounded, shape(rows, 128, jnp.float32)] * 2
    outs.append(shape(2 * rows, width, jnp.bfloat16))
    return call(
        functools.partial(prepare_kernel, start),
        outs,
        [SMEM, HBM, HBM],
        [VMEM] * len(outs),
        [pltpu.SemaphoreType.DMA((2, rows // TILE))],
        limit=50,
    )(even, images, texts)


def coefficients(scale, bias, left, right, diagonal=False):
    logits = scale * lax.dot_general(
        left, right, (((1,), (1,)), ((), ())), preferred_element_type=jnp.float32
    ) + bias
    if diagonal:
        here = lax.broadcasted_iota(jnp.int32, logits.shape, 0) == lax.broadcasted_iota(
            jnp.int32, logits.shape, 1
        )
        logits = jnp.where(here, -logits, logits)
        factor = jnp.where(here, -scale, scale)
    else:
        factor = scale
    return (factor / (1.0 + jnp.exp(-logits))).astype(jnp.bfloat16)


def product(coef, right):
    return jnp.dot(coef, right, preferred_element_type=jnp.float32)


def own_kernel(
    scalars, first1, first2, second1, second2,
    raw11, raw12, raw21, raw22, norm11, norm12, norm21, norm22,
    total1, total2, unit1, unit2, size1, size2,
):
    scale, bias = scalars[0], scalars[1]
    firsts, seconds = (first1, first2), (second1, second2)
    rows = first1.shape[0]
    for lefts, rights, total in ((firsts, seconds, total1), (seconds, firsts, total2)):
        for i, left in enumerate(lefts):
            at = pl.ds(i * rows, rows)
            for j, right in enumerate(rights):
                term = product(coefficients(scale, bias, left[...], right[...], i == j), right[...])
                total[at] = term if j == 0 else total[at] + term
    for raws, norms, unit, size in (
        ((raw11, raw12), (norm11, norm12), unit1, size1),
        ((raw21, raw22), (norm21, norm22), unit2, size2),
    ):
        for i in range(2):
            at = pl.ds(i * rows, rows)
            unit[at] = raws[i][...].astype(jnp.float32) * norms[i][:, :1]
            size[at] = norms[i][...]


def add_kernel(scalars, first1, first2, second1, second2, in1, in2, right1, right2, total1, total2):
    scale, bias = scalars[0], scalars[1]
    rows = first1.shape[0]
    for lefts, right, given, total in (
        ((first1, first2), right1, in1, total1),
        ((second1, second2), right2, in2, total2),
    ):
        for i, left in enumerate(lefts):
            at = pl.ds(i * rows, rows)
            total[at] = given[at] + product(coefficients(scale, bias, left[...], right[...]), right[...])


def cross_kernel(scalars, first1, first2, second1, second2, in1, in2, both, total1, total2):
    rows = first1.shape[0]
    add_kernel(
        scalars, first1, first2, second1, second2, in1, in2,
        both.at[pl.ds(rows, rows)], both.at[pl.ds(0, rows)], total1, total2,
    )


def last_kernel(
    slot, scalars, even, left1, left2, right, given, unit, norm, image_in, text_in,
    image_grad, text_grad, out, sems,
):
    del image_in, text_in
    scale, bias = scalars[0], scalars[1]
    rows = left1.shape[0]

    def give(tile, target):
        at = pl.ds(tile * TILE, TILE)
        return pltpu.make_async_copy(out.at[at], target.at[at], sems.at[tile])

    coefs = [coefficients(scale, bias, left[...], right[...]) for left in (left1, left2)]
    tiles = 2 * rows // TILE
    for tile in range(tiles):
        i, inner = divmod(tile * TILE, rows)
        at = pl.ds(tile * TILE, TILE)
        whole = given[at] + product(coefs[i][inner : inner + TILE], right[...])
        along = jnp.sum(unit[at] * whole, axis=-1, keepdims=True)
        out[at] = ((whole - unit[at] * along) * norm[at][:, :1]).astype(jnp.bfloat16)

        @pl.when((even[0] == 1) == (slot == 0))
        def _():
            give(tile, text_grad).start()

        @pl.when((even[0] == 1) != (slot == 0))
        def _():
            give(tile, image_grad).start()

    for tile in range(tiles):
        give(tile, text_grad).wait()


def first_last_kernel(scalars, even, left1, left2, right, given, unit, norm, *refs):
    last_kernel(0, scalars, even, left1, left2, right, given, unit, norm, None, None, *refs)


def on_device(images, texts, logit_scale, logit_bias):
    rows, width = images.shape
    near, far, cross = routes(lax.axis_size("grp"), lax.axis_size("blk"))
    even = (1 - lax.axis_index("blk") % 2).astype(jnp.int32).reshape(1)
    scalars = jnp.concatenate([logit_scale, logit_bias])

    half = rows // 2
    first1, raw11, norm11, second1, raw21, norm21, both1 = prepare(
        0, half, even, images, texts
    )
    first2, raw12, norm12, second2, raw22, norm22, both2 = prepare(
        half, half, even, images, texts
    )

    def send(block, route):
        return lax.ppermute(block, AXES, route)

    blocks = (first1, first2, second1, second2)
    totals = [shape(rows, width, jnp.float32)] * 2

    def add(body, total1, total2, *rights):
        return call(
            body, totals, [SMEM] + [VMEM] * (6 + len(rights)), [VMEM] * 2, aliases={5: 0, 6: 1}
        )(scalars, *blocks, total1, total2, *rights)

    far_a, near_a = send(second1, far), send(first1, near)
    far_b, near_b = send(second2, far), send(first2, near)
    cross1 = send(both1, cross)
    units = totals + [shape(rows, 128, jnp.float32)] * 2
    total1, total2, unit1, unit2, size1, size2 = call(
        own_kernel, totals + units, [SMEM] + [VMEM] * 12, [VMEM] * 6
    )(scalars, *blocks, raw11, raw12, raw21, raw22, norm11, norm12, norm21, norm22)
    total1, total2 = add(cross_kernel, total1, total2, cross1)
    near_a, far_a, total1, total2, both2 = lax.optimization_barrier(
        (near_a, far_a, total1, total2, both2)
    )
    far_next_a, near_next_a = send(near_a, far), send(far_a, near)
    cross2 = send(both2, cross)
    total1, total2 = add(add_kernel, total1, total2, near_a, far_a)
    near_b, far_b, total1, total2 = lax.optimization_barrier((near_b, far_b, total1, total2))
    far_next_b, near_next_b = send(near_b, far), send(far_b, near)
    total1, total2 = add(add_kernel, total1, total2, near_b, far_b)
    total1, total2 = add(add_kernel, total1, total2, near_next_a, far_next_a)
    total1, total2 = add(cross_kernel, total1, total2, cross2)

    def last(body, given, *operands):
        return call(
            body,
            [shape(rows, width, jnp.bfloat16)] * 2,
            [SMEM] * 2 + [VMEM] * 6 + [HBM] * given,
            [HBM] * 2,
            [pltpu.VMEM((rows, width), jnp.bfloat16), pltpu.SemaphoreType.DMA((rows // TILE,))],
            aliases={8: 0, 9: 1} if given else None,
        )(scalars, even, *operands)

    grads = last(first_last_kernel, 0, first1, first2, near_next_b, total1, unit1, size1)
    return last(
        functools.partial(last_kernel, 1), 2, second1, second2, far_next_b, total2, unit2, size2, *grads
    )


def solution(mesh):
    spec = P(AXES, None)
    return jax.shard_map(
        on_device,
        mesh=mesh,
        in_specs=(spec, spec, P(), P()),
        out_specs=(spec, spec),
        check_vma=False,
    )
```

time: 106 us -> 69.3 us (0.65)
  the two profiles are of different devices: /device:TPU:2 before, /device:TPU:1 now
where the time goes in v2:
time: 69.3 us; the launch traced here: 69.2 us
  Pallas kernels  30.7 us (44%)
  starting transfers between devices  29.3 us (42%)
  waiting for transfers between devices  6.94 us (10%)
  between operations  2.22 us (3%)
    ppermute x10, starting transfers between devices, send(): return lax.ppermute(block, AXES, route)  29.3 us
    pallas_call x5, Pallas kernels, add(): call(body, totals, [SMEM] + [VMEM] * (6 + len(rights)), [VMEM] * 2, alias...  16 us
    ppermute x10, waiting for transfers between devices, send(): return lax.ppermute(block, AXES, route)  6.94 us
    pallas_call x1, Pallas kernels, on_device(): call(own_kernel, totals + units, [SMEM] + [VMEM] * 12, [VMEM] * 6)  5.74 us
    pallas_call x2, Pallas kernels, last(): call(body, [shape(rows, width, jnp.bfloat16)] * 2, [SMEM] * 2 + [VMEM] *...  5.67 us
    pallas_call x2, Pallas kernels, prepare(): call(functools.partial(prepare_kernel, start), outs, [SMEM, HBM, HBM], [V...  3.3 us
  transfers between devices with their start and end apart: 10, of which 4 were waited for; matrix products, arithmetic and copies ran while one was open for 0% of the time, Pallas kernels for 38%

profile of v2, /device:TPU:1, one launch (start us, length us, event | category | flops | bytes accessed | tf_op | source)
XLA Modules:
  0.0 69.2 jit_solution(5654097127466153934)
XLA Ops:
  0.6 1.7 %shard_map.59 = (bf16[256,1152]{1,0:T(8,128)(2,1)S(1)}, bf16[256,1152]{1,0:T(8,128)(2,1)S(1)}, f32[256,128]{1,0:T(8,128)S(1)}, bf16[256,1152]{1,0:T(8,128)(2,1)S...) custom-call(s32[1]{0:T(128)} %bitcast.even, bf16[512,1152]{1,0:T(8,128)(2,1)} %images.3, ...), custom_call_target="tpu_custom_call" | custom-call | tf_op jit(solution)/shard_map/pallas_call | solution.py:91
  2.3 3.3 %collective-permute-start.4 = (bf16[512,1152]{1,0:T(8,128)(2,1)S(1)}, bf16[512,1152]{1,0:T(8,128)(2,1)S(1)}, u32[]{:S(2)}, u32[]{:S(2)}) collective-permute-start(bf16[512,1152]{1,0:T(8,128)(2,1)S(1)} %get-tuple-element.57), channel_id=1, source_target_pairs={{0,64},{1,65},{2,66},{3,67},{4,68},{5,69},{6,70},{7,71},{8,72},{9,... | collective-permute-start | bytes 3538952 | tf_op jit(solution)/shard_map/ppermute | solution.py:216
  5.6 0.0 collective-permute-start.2
  5.6 9.2 %collective-permute-start.3 = (bf16[256,1152]{1,0:T(8,128)(2,1)S(1)}, bf16[256,1152]{1,0:T(8,128)(2,1)S(1)}, u32[]{:S(2)}, u32[]{:S(2)}) collective-permute-start(bf16[256,1152]{1,0:T(8,128)(2,1)S(1)} %get-tuple-element.43.second1.left1), channel_id=1, source_target_pairs={{0,63},{1,2},{2,1},{3,4},{4,3},{5,6},{6,5},{7,8},{8,7},{9,10},{10,... | collective-permute-start | bytes 1769480 | tf_op jit(solution)/shard_map/ppermute | solution.py:216
  14.9 1.6 %shard_map.60 = (bf16[256,1152]{1,0:T(8,128)(2,1)S(1)}, bf16[256,1152]{1,0:T(8,128)(2,1)S(1)}, f32[256,128]{1,0:T(8,128)S(1)}, bf16[256,1152]{1,0:T(8,128)(2,1)S...) custom-call(s32[1]{0:T(128)} %bitcast.even, bf16[512,1152]{1,0:T(8,128)(2,1)} %images.3, ...), custom_call_target="tpu_custom_call" | custom-call | tf_op jit(solution)/shard_map/pallas_call | solution.py:91
  16.5 0.1 collective-permute-start
  16.6 0.9 %collective-permute-start.1 = (bf16[256,1152]{1,0:T(8,128)(2,1)S(1)}, bf16[256,1152]{1,0:T(8,128)(2,1)S(1)}, u32[]{:S(2)}, u32[]{:S(2)}) collective-permute-start(bf16[256,1152]{1,0:T(8,128)(2,1)S(1)} %get-tuple-element.44.second2.left2), channel_id=1, source_target_pairs={{0,63},{1,2},{2,1},{3,4},{4,3},{5,6},{6,5},{7,8},{8,7},{9,10},{10,... | collective-permute-start | bytes 1769480 | tf_op jit(solution)/shard_map/ppermute | solution.py:216
  18.8 0.1 pad_maximum_fusion.scalars
  18.9 5.7 %shard_map.61 = (f32[512,1152]{1,0:T(8,128)S(1)}, f32[512,1152]{1,0:T(8,128)S(1)}, f32[512,1152]{1,0:T(8,128)S(1)}, f32[512,1152]{1,0:T(8,128)S(1)}, f32[512,128]{1,0:T(8,128)S(1)}, /*index=5*/f32[512,128]{1,0:T(8,128)S(1)}) custom-call(f32[2]{0:T(128)S(1)} %pad_maximum_fusion.scalars, bf16[256,1152]{1,0:T(8,128)(2,1)S(1)} %get-tuple-element.46.first1.left1, ...), custom_call_target="tpu_custom_call" | custom-call | tf_op jit(solution)/shard_map/pallas_call | solution.py:230
  24.6 0.0 collective-permute-done.4.both
  24.7 3.2 %shard_map.62 = (f32[512,1152]{1,0:T(8,128)S(1)}, f32[512,1152]{1,0:T(8,128)S(1)}) custom-call(f32[2]{0:T(128)S(1)} %pad_maximum_fusion.scalars, bf16[256,1152]{1,0:T(8,128)(2,1)S(1)} %get-tuple-element.46.first1.left1, bf16[256,1152]{1,0:T(8,128)(2,1)S(1)} %get-tuple-element.45.first2.left2, ...), custom_call_target="tpu_custom_call", output_to_operand_aliasing={{0}: (5, {}), {1}: (6, {})} | custom-call | tf_op jit(solution)/shard_map/pallas_call | solution.py:222
  27.9 0.0 collective-permute-done.2.right1
  27.9 0.4 collective-permute-done.3.right2
  28.3 1.3 %collective-permute-start.8 = (bf16[512,1152]{1,0:T(8,128)(2,1)S(1)}, bf16[512,1152]{1,0:T(8,128)(2,1)S(1)}, u32[]{:S(2)}, u32[]{:S(2)}) collective-permute-start(bf16[512,1152]{1,0:T(8,128)(2,1)S(1)} %get-tuple-element.75), channel_id=1, source_target_pairs={{0,64},{1,65},{2,66},{3,67},{4,68},{5,69},{6,70},{7,71},{8,72},{9,... | collective-permute-start | bytes 3538952 | tf_op jit(solution)/shard_map/ppermute | solution.py:216
  29.6 0.0 collective-permute-start.6
  29.6 7.5 %collective-permute-start.7 = (bf16[256,1152]{1,0:T(8,128)(2,1)S(1)}, bf16[256,1152]{1,0:T(8,128)(2,1)S(1)}, u32[]{:S(2)}, u32[]{:S(2)}) collective-permute-start(bf16[256,1152]{1,0:T(8,128)(2,1)S(1)} %collective-permute-done.2.right1), channel_id=1, source_target_pairs={{0,63},{1,2},{2,1},{3,4},{4,3},{5,6},{6,5},{7,8},{8,7},{9,10},{10,... | collective-permute-start | bytes 1769480 | tf_op jit(solution)/shard_map/ppermute | solution.py:216
  37.1 3.2 %shard_map.63 = (f32[512,1152]{1,0:T(8,128)S(1)}, f32[512,1152]{1,0:T(8,128)S(1)}) custom-call(f32[2]{0:T(128)S(1)} %pad_maximum_fusion.scalars, bf16[256,1152]{1,0:T(8,128)(2,1)S(1)} %get-tuple-element.46.first1.left1, bf16[256,1152]{1,0:T(8,128)(2,1)S(1)} %get-tuple-element.45.first2.left2, ...), custom_call_target="tpu_custom_call", output_to_operand_aliasing={{0}: (5, {}), {1}: (6, {})} | custom-call | tf_op jit(solution)/shard_map/pallas_call | solution.py:222
  40.3 0.0 collective-permute-done.right1
  40.3 0.6 collective-permute-done.1.right2
  40.9 0.0 collective-permute-start.9
  40.9 6.9 %collective-permute-start.5 = (bf16[256,1152]{1,0:T(8,128)(2,1)S(1)}, bf16[256,1152]{1,0:T(8,128)(2,1)S(1)}, u32[]{:S(2)}, u32[]{:S(2)}) collective-permute-start(bf16[256,1152]{1,0:T(8,128)(2,1)S(1)} %collective-permute-done.right1), channel_id=1, source_target_pairs={{0,63},{1,2},{2,1},{3,4},{4,3},{5,6},{6,5},{7,8},{8,7},{9,10},{10,... | collective-permute-start | bytes 1769480 | tf_op jit(solution)/shard_map/ppermute | solution.py:216
  47.8 3.2 %shard_map.64 = (f32[512,1152]{1,0:T(8,128)S(1)}, f32[512,1152]{1,0:T(8,128)S(1)}) custom-call(f32[2]{0:T(128)S(1)} %pad_maximum_fusion.scalars, bf16[256,1152]{1,0:T(8,128)(2,1)S(1)} %get-tuple-element.46.first1.left1, bf16[256,1152]{1,0:T(8,128)(2,1)S(1)} %get-tuple-element.45.first2.left2, ...), custom_call_target="tpu_custom_call", output_to_operand_aliasing={{0}: (5, {}), {1}: (6, {})} | custom-call | tf_op jit(solution)/shard_map/pallas_call | solution.py:222
  51.0 0.0 collective-permute-done.6.right1
  51.0 2.5 %collective-permute-done.7.right2 = bf16[256,1152]{1,0:T(8,128)(2,1)S(1)} collective-permute-done((bf16[256,1152]{1,0:T(8,128)(2,1)S(1)}, bf16[256,1152]{1,0:T(8,128)(2,1)S(1)}, u32[]{:S(2)}, u32[]{:S(2)}) %collective-permute-start.7) | collective-permute-done | bytes 589856 | tf_op jit(solution)/shard_map/ppermute | solution.py:216
  53.6 3.2 %shard_map.65 = (f32[512,1152]{1,0:T(8,128)S(1)}, f32[512,1152]{1,0:T(8,128)S(1)}) custom-call(f32[2]{0:T(128)S(1)} %pad_maximum_fusion.scalars, bf16[256,1152]{1,0:T(8,128)(2,1)S(1)} %get-tuple-element.46.first1.left1, bf16[256,1152]{1,0:T(8,128)(2,1)S(1)} %get-tuple-element.45.first2.left2, ...), custom_call_target="tpu_custom_call", output_to_operand_aliasing={{0}: (5, {}), {1}: (6, {})} | custom-call | tf_op jit(solution)/shard_map/pallas_call | solution.py:222
  56.7 0.0 collective-permute-done.8.both
  56.8 3.2 %shard_map.66 = (f32[512,1152]{1,0:T(8,128)S(1)}, f32[512,1152]{1,0:T(8,128)S(1)}) custom-call(f32[2]{0:T(128)S(1)} %pad_maximum_fusion.scalars, bf16[256,1152]{1,0:T(8,128)(2,1)S(1)} %get-tuple-element.46.first1.left1, bf16[256,1152]{1,0:T(8,128)(2,1)S(1)} %get-tuple-element.45.first2.left2, ...), custom_call_target="tpu_custom_call", output_to_operand_aliasing={{0}: (5, {}), {1}: (6, {})} | custom-call | tf_op jit(solution)/shard_map/pallas_call | solution.py:222
  59.9 0.0 collective-permute-done.9.right
  60.0 2.8 %shard_map.67 = (bf16[512,1152]{1,0:T(8,128)(2,1)}, bf16[512,1152]{1,0:T(8,128)(2,1)}) custom-call(f32[2]{0:T(128)S(1)} %pad_maximum_fusion.scalars, s32[1]{0:T(128)} %bitcast.even, bf16[256,1152]{1,0:T(8,128)(2,1)S(1)} %get-tuple-element.46.first1.left1, bf16[256,1152]{1,0:T(8,128)(2,1)S(1)} %get-tuple-element.45.first2.left2, ...), custom_call_target="tpu_custom_call" | custom-call | tf_op jit(solution)/shard_map/pallas_call | solution.py:247
  62.8 3.4 %collective-permute-done.5.right = bf16[256,1152]{1,0:T(8,128)(2,1)S(1)} collective-permute-done((bf16[256,1152]{1,0:T(8,128)(2,1)S(1)}, bf16[256,1152]{1,0:T(8,128)(2,1)S(1)}, u32[]{:S(2)}, u32[]{:S(2)}) %collective-permute-start.5) | collective-permute-done | bytes 589856 | tf_op jit(solution)/shard_map/ppermute | solution.py:216
  66.2 2.8 %shard_map.68 = (bf16[512,1152]{1,0:T(8,128)(2,1)}, bf16[512,1152]{1,0:T(8,128)(2,1)}) custom-call(f32[2]{0:T(128)S(1)} %pad_maximum_fusion.scalars, s32[1]{0:T(128)} %bitcast.even, bf16[256,1152]{1,0:T(8,128)(2,1)S(1)} %get-tuple-element.43.second1.left1, ...), custom_call_target="tpu_custom_call", output_to_operand_aliasing={{0}: (8, {}), {1}: (9, {})} | custom-call | tf_op jit(solution)/shard_map/pallas_call | solution.py:247
Async XLA Ops:
  2.3 22.3 %collective-permute-start.4 = (bf16[512,1152]{1,0:T(8,128)(2,1)S(1)}, bf16[512,1152]{1,0:T(8,128)(2,1)S(1)}, u32[]{:S(2)}, u32[]{:S(2)}) collective-permute-start(bf16[512,1152]{1,0:T(8,128)(2,1)S(1)} %get-tuple-element.57), channel_id=1, source_target_pairs={{0,64},{1,65},{2,66},{3,67},{4,68},{5,69},{6,70},{7,71},{8,72},{9,... | collective-permute-start | bytes 3538952 | tf_op jit(solution)/shard_map/ppermute | solution.py:216
  5.6 22.2 %collective-permute-start.2 = (bf16[256,1152]{1,0:T(8,128)(2,1)S(1)}, bf16[256,1152]{1,0:T(8,128)(2,1)S(1)}, u32[]{:S(2)}, u32[]{:S(2)}) collective-permute-start(bf16[256,1152]{1,0:T(8,128)(2,1)S(1)} %get-tuple-element.46.first1.left1), channel_id=1, source_target_pairs={{0,1},{1,0},{2,3},{3,2},{4,5},{5,4},{6,7},{7,6},{8,9},{9,8},{10,11... | collective-permute-start | bytes 1769480 | tf_op jit(solution)/shard_map/ppermute | solution.py:216
  5.6 22.6 %collective-permute-start.3 = (bf16[256,1152]{1,0:T(8,128)(2,1)S(1)}, bf16[256,1152]{1,0:T(8,128)(2,1)S(1)}, u32[]{:S(2)}, u32[]{:S(2)}) collective-permute-start(bf16[256,1152]{1,0:T(8,128)(2,1)S(1)} %get-tuple-element.43.second1.left1), channel_id=1, source_target_pairs={{0,63},{1,2},{2,1},{3,4},{4,3},{5,6},{6,5},{7,8},{8,7},{9,10},{10,... | collective-permute-start | bytes 1769480 | tf_op jit(solution)/shard_map/ppermute | solution.py:216
  16.5 23.8 %collective-permute-start = (bf16[256,1152]{1,0:T(8,128)(2,1)S(1)}, bf16[256,1152]{1,0:T(8,128)(2,1)S(1)}, u32[]{:S(2)}, u32[]{:S(2)}) collective-permute-start(bf16[256,1152]{1,0:T(8,128)(2,1)S(1)} %get-tuple-element.45.first2.left2), channel_id=1, source_target_pairs={{0,1},{1,0},{2,3},{3,2},{4,5},{5,4},{6,7},{7,6},{8,9},{9,8},{10,11... | collective-permute-start | bytes 1769480 | tf_op jit(solution)/shard_map/ppermute | solution.py:216
  16.6 24.3 %collective-permute-start.1 = (bf16[256,1152]{1,0:T(8,128)(2,1)S(1)}, bf16[256,1152]{1,0:T(8,128)(2,1)S(1)}, u32[]{:S(2)}, u32[]{:S(2)}) collective-permute-start(bf16[256,1152]{1,0:T(8,128)(2,1)S(1)} %get-tuple-element.44.second2.left2), channel_id=1, source_target_pairs={{0,63},{1,2},{2,1},{3,4},{4,3},{5,6},{6,5},{7,8},{8,7},{9,10},{10,... | collective-permute-start | bytes 1769480 | tf_op jit(solution)/shard_map/ppermute | solution.py:216
  28.3 28.5 %collective-permute-start.8 = (bf16[512,1152]{1,0:T(8,128)(2,1)S(1)}, bf16[512,1152]{1,0:T(8,128)(2,1)S(1)}, u32[]{:S(2)}, u32[]{:S(2)}) collective-permute-start(bf16[512,1152]{1,0:T(8,128)(2,1)S(1)} %get-tuple-element.75), channel_id=1, source_target_pairs={{0,64},{1,65},{2,66},{3,67},{4,68},{5,69},{6,70},{7,71},{8,72},{9,... | collective-permute-start | bytes 3538952 | tf_op jit(solution)/shard_map/ppermute | solution.py:216
  29.6 21.4 %collective-permute-start.6 = (bf16[256,1152]{1,0:T(8,128)(2,1)S(1)}, bf16[256,1152]{1,0:T(8,128)(2,1)S(1)}, u32[]{:S(2)}, u32[]{:S(2)}) collective-permute-start(bf16[256,1152]{1,0:T(8,128)(2,1)S(1)} %collective-permute-done.3.right2), channel_id=1, source_target_pairs={{0,1},{1,0},{2,3},{3,2},{4,5},{5,4},{6,7},{7,6},{8,9},{9,8},{10,11... | collective-permute-start | bytes 1769480 | tf_op jit(solution)/shard_map/ppermute | solution.py:216
  29.6 23.9 %collective-permute-start.7 = (bf16[256,1152]{1,0:T(8,128)(2,1)S(1)}, bf16[256,1152]{1,0:T(8,128)(2,1)S(1)}, u32[]{:S(2)}, u32[]{:S(2)}) collective-permute-start(bf16[256,1152]{1,0:T(8,128)(2,1)S(1)} %collective-permute-done.2.right1), channel_id=1, source_target_pairs={{0,63},{1,2},{2,1},{3,4},{4,3},{5,6},{6,5},{7,8},{8,7},{9,10},{10,... | collective-permute-start | bytes 1769480 | tf_op jit(solution)/shard_map/ppermute | solution.py:216
  40.9 19.0 %collective-permute-start.9 = (bf16[256,1152]{1,0:T(8,128)(2,1)S(1)}, bf16[256,1152]{1,0:T(8,128)(2,1)S(1)}, u32[]{:S(2)}, u32[]{:S(2)}) collective-permute-start(bf16[256,1152]{1,0:T(8,128)(2,1)S(1)} %collective-permute-done.1.right2), channel_id=1, source_target_pairs={{0,1},{1,0},{2,3},{3,2},{4,5},{5,4},{6,7},{7,6},{8,9},{9,8},{10,11... | collective-permute-start | bytes 1769480 | tf_op jit(solution)/shard_map/ppermute | solution.py:216
  40.9 25.3 %collective-permute-start.5 = (bf16[256,1152]{1,0:T(8,128)(2,1)S(1)}, bf16[256,1152]{1,0:T(8,128)(2,1)S(1)}, u32[]{:S(2)}, u32[]{:S(2)}) collective-permute-start(bf16[256,1152]{1,0:T(8,128)(2,1)S(1)} %collective-permute-done.right1), channel_id=1, source_target_pairs={{0,63},{1,2},{2,1},{3,4},{4,3},{5,6},{6,5},{7,8},{8,7},{9,10},{10,... | collective-permute-start | bytes 1769480 | tf_op jit(solution)/shard_map/ppermute | solution.py:216

commit v3 on v2

--- a/solution.py
+++ b/solution.py
@@ -75,8 +75,7 @@
         for slot, (half, raw, norm) in enumerate(blocks):
             fetch(slot, images, tile).wait()
             values = raw[at].astype(jnp.float32)
-            size = jnp.sqrt(jnp.sum(values * values, axis=-1, keepdims=True) + 1e-06)
-            inverse = 1.0 / size
+            inverse = lax.rsqrt(jnp.sum(values * values, axis=-1, keepdims=True) + 1e-06)
             rounded = (values * inverse).astype(jnp.bfloat16)
             half[at] = rounded
             both[pl.ds(slot * rows + tile * TILE, TILE)] = rounded
@@ -99,18 +98,15 @@
 
 
 def coefficients(scale, bias, left, right, diagonal=False):
-    logits = scale * lax.dot_general(
-        left, right, (((1,), (1,)), ((), ())), preferred_element_type=jnp.float32
-    ) + bias
-    if diagonal:
-        here = lax.broadcasted_iota(jnp.int32, logits.shape, 0) == lax.broadcasted_iota(
-            jnp.int32, logits.shape, 1
-        )
-        logits = jnp.where(here, -logits, logits)
-        factor = jnp.where(here, -scale, scale)
-    else:
-        factor = scale
-    return (factor / (1.0 + jnp.exp(-logits))).astype(jnp.bfloat16)
+    dots = lax.dot_general(left, right, (((1,), (1,)), ((), ())), preferred_element_type=jnp.float32)
+    power = dots * (-scale) - bias
+    if not diagonal:
+        return (scale / (1.0 + jnp.exp(power))).astype(jnp.bfloat16)
+    here = lax.broadcasted_iota(jnp.int32, dots.shape, 0) == lax.broadcasted_iota(
+        jnp.int32, dots.shape, 1
+    )
+    factor = jnp.where(here, -scale, scale)
+    return (factor / (1.0 + jnp.exp(jnp.where(here, -power, power)))).astype(jnp.bfloat16)
 
 
 def product(coef, right):
@@ -230,12 +226,12 @@
     total1, total2, unit1, unit2, size1, size2 = call(
         own_kernel, totals + units, [SMEM] + [VMEM] * 12, [VMEM] * 6
     )(scalars, *blocks, raw11, raw12, raw21, raw22, norm11, norm12, norm21, norm22)
-    total1, total2 = add(cross_kernel, total1, total2, cross1)
     near_a, far_a, total1, total2, both2 = lax.optimization_barrier(
         (near_a, far_a, total1, total2, both2)
     )
     far_next_a, near_next_a = send(near_a, far), send(far_a, near)
     cross2 = send(both2, cross)
+    total1, total2 = add(cross_kernel, total1, total2, cross1)
     total1, total2 = add(add_kernel, total1, total2, near_a, far_a)
     near_b, far_b, total1, total2 = lax.optimization_barrier((near_b, far_b, total1, total2))
     far_next_b, near_next_b = send(near_b, far), send(far_b, near)

time: 69.3 us -> 69.3 us (level)
  waiting for transfers between devices: 6.94 us -> 9.68 us
  starting transfers between devices: 29.3 us -> 26.6 us
    ppermute x10, waiting for transfers between devices: 6.94 us -> 9.68 us  [send(): return lax.ppermute(block, AXES, route)]
    ppermute x10, starting transfers between devices: 29.3 us -> 26.6 us  [send(): return lax.ppermute(block, AXES, route)]
  transfers between devices with their start and end apart: 10 -> 10, of which waited for: 4 -> 3; matrix products, arithmetic and copies ran while one was open for 0% -> 0% of each run, Pallas kernels for 38% -> 38%
where the time goes in v3:
time: 69.3 us; the launch traced here: 69.1 us
  Pallas kernels  30.5 us (44%)
  starting transfers between devices  26.6 us (38%)
  waiting for transfers between devices  9.68 us (14%)
  between operations  2.22 us (3%)
    ppermute x10, starting transfers between devices, send(): return lax.ppermute(block, AXES, route)  26.6 us
    pallas_call x5, Pallas kernels, add(): call(body, totals, [SMEM] + [VMEM] * (6 + len(rights)), [VMEM] * 2, alias...  16 us
    ppermute x10, waiting for transfers between devices, send(): return lax.ppermute(block, AXES, route)  9.68 us
    pallas_call x1, Pallas kernels, on_device(): call(own_kernel, totals + units, [SMEM] + [VMEM] * 12, [VMEM] * 6)  5.69 us
    pallas_call x2, Pallas kernels, last(): call(body, [shape(rows, width, jnp.bfloat16)] * 2, [SMEM] * 2 + [VMEM] *...  5.63 us
    pallas_call x2, Pallas kernels, prepare(): call(functools.partial(prepare_kernel, start), outs, [SMEM, HBM, HBM], [V...  3.18 us
  transfers between devices with their start and end apart: 10, of which 3 were waited for; matrix products, arithmetic and copies ran while one was open for 0% of the time, Pallas kernels for 38%

profile of v3, /device:TPU:1, one launch (start us, length us, event | category | flops | bytes accessed | tf_op | source)
XLA Modules:
  0.0 69.1 jit_solution(3872244095072629803)
XLA Ops:
  0.6 1.6 %shard_map.59 = (bf16[256,1152]{1,0:T(8,128)(2,1)S(1)}, bf16[256,1152]{1,0:T(8,128)(2,1)S(1)}, f32[256,128]{1,0:T(8,128)S(1)}, bf16[256,1152]{1,0:T(8,128)(2,1)S...) custom-call(s32[1]{0:T(128)} %bitcast.even, bf16[512,1152]{1,0:T(8,128)(2,1)} %images.3, ...), custom_call_target="tpu_custom_call" | custom-call | tf_op jit(solution)/shard_map/pallas_call | solution.py:90
  2.2 3.3 %collective-permute-start.4 = (bf16[512,1152]{1,0:T(8,128)(2,1)S(1)}, bf16[512,1152]{1,0:T(8,128)(2,1)S(1)}, u32[]{:S(2)}, u32[]{:S(2)}) collective-permute-start(bf16[512,1152]{1,0:T(8,128)(2,1)S(1)} %get-tuple-element.60), channel_id=1, source_target_pairs={{0,64},{1,65},{2,66},{3,67},{4,68},{5,69},{6,70},{7,71},{8,72},{9,... | collective-permute-start | bytes 3538952 | tf_op jit(solution)/shard_map/ppermute | solution.py:212
  5.6 0.0 collective-permute-start.2
  5.6 9.2 %collective-permute-start.3 = (bf16[256,1152]{1,0:T(8,128)(2,1)S(1)}, bf16[256,1152]{1,0:T(8,128)(2,1)S(1)}, u32[]{:S(2)}, u32[]{:S(2)}) collective-permute-start(bf16[256,1152]{1,0:T(8,128)(2,1)S(1)} %get-tuple-element.43.second1.left1), channel_id=1, source_target_pairs={{0,63},{1,2},{2,1},{3,4},{4,3},{5,6},{6,5},{7,8},{8,7},{9,10},{10,... | collective-permute-start | bytes 1769480 | tf_op jit(solution)/shard_map/ppermute | solution.py:212
  14.8 1.6 %shard_map.60 = (bf16[256,1152]{1,0:T(8,128)(2,1)S(1)}, bf16[256,1152]{1,0:T(8,128)(2,1)S(1)}, f32[256,128]{1,0:T(8,128)S(1)}, bf16[256,1152]{1,0:T(8,128)(2,1)S...) custom-call(s32[1]{0:T(128)} %bitcast.even, bf16[512,1152]{1,0:T(8,128)(2,1)} %images.3, ...), custom_call_target="tpu_custom_call" | custom-call | tf_op jit(solution)/shard_map/pallas_call | solution.py:90
  16.4 0.1 collective-permute-start
  16.5 0.9 %collective-permute-start.1 = (bf16[256,1152]{1,0:T(8,128)(2,1)S(1)}, bf16[256,1152]{1,0:T(8,128)(2,1)S(1)}, u32[]{:S(2)}, u32[]{:S(2)}) collective-permute-start(bf16[256,1152]{1,0:T(8,128)(2,1)S(1)} %get-tuple-element.44.second2.left2), channel_id=1, source_target_pairs={{0,63},{1,2},{2,1},{3,4},{4,3},{5,6},{6,5},{7,8},{8,7},{9,10},{10,... | collective-permute-start | bytes 1769480 | tf_op jit(solution)/shard_map/ppermute | solution.py:212
  18.7 0.1 pad_maximum_fusion.scalars
  18.8 5.7 %shard_map.61 = (f32[512,1152]{1,0:T(8,128)S(1)}, f32[512,1152]{1,0:T(8,128)S(1)}, f32[512,1152]{1,0:T(8,128)S(1)}, f32[512,1152]{1,0:T(8,128)S(1)}, f32[512,128]{1,0:T(8,128)S(1)}, /*index=5*/f32[512,128]{1,0:T(8,128)S(1)}) custom-call(f32[2]{0:T(128)S(1)} %pad_maximum_fusion.scalars, bf16[256,1152]{1,0:T(8,128)(2,1)S(1)} %get-tuple-element.46.first1.left1, ...), custom_call_target="tpu_custom_call" | custom-call | tf_op jit(solution)/shard_map/pallas_call | solution.py:226
  24.5 0.0 collective-permute-done.2.right1
  24.5 3.7 %collective-permute-done.3.right2 = bf16[256,1152]{1,0:T(8,128)(2,1)S(1)} collective-permute-done((bf16[256,1152]{1,0:T(8,128)(2,1)S(1)}, bf16[256,1152]{1,0:T(8,128)(2,1)S(1)}, u32[]{:S(2)}, u32[]{:S(2)}) %collective-permute-start.3) | collective-permute-done | bytes 589856 | tf_op jit(solution)/shard_map/ppermute | solution.py:212
  28.2 1.3 %collective-permute-start.8 = (bf16[512,1152]{1,0:T(8,128)(2,1)S(1)}, bf16[512,1152]{1,0:T(8,128)(2,1)S(1)}, u32[]{:S(2)}, u32[]{:S(2)}) collective-permute-start(bf16[512,1152]{1,0:T(8,128)(2,1)S(1)} %get-tuple-element.75), channel_id=1, source_target_pairs={{0,64},{1,65},{2,66},{3,67},{4,68},{5,69},{6,70},{7,71},{8,72},{9,... | collective-permute-start | bytes 3538952 | tf_op jit(solution)/shard_map/ppermute | solution.py:212
  29.6 0.0 collective-permute-start.6
  29.6 0.0 collective-permute-done.4.both
  29.6 7.5 %collective-permute-start.7 = (bf16[256,1152]{1,0:T(8,128)(2,1)S(1)}, bf16[256,1152]{1,0:T(8,128)(2,1)S(1)}, u32[]{:S(2)}, u32[]{:S(2)}) collective-permute-start(bf16[256,1152]{1,0:T(8,128)(2,1)S(1)} %collective-permute-done.2.right1), channel_id=1, source_target_pairs={{0,63},{1,2},{2,1},{3,4},{4,3},{5,6},{6,5},{7,8},{8,7},{9,10},{10,... | collective-permute-start | bytes 1769480 | tf_op jit(solution)/shard_map/ppermute | solution.py:212
  37.1 3.2 %shard_map.62 = (f32[512,1152]{1,0:T(8,128)S(1)}, f32[512,1152]{1,0:T(8,128)S(1)}) custom-call(f32[2]{0:T(128)S(1)} %pad_maximum_fusion.scalars, bf16[256,1152]{1,0:T(8,128)(2,1)S(1)} %get-tuple-element.46.first1.left1, bf16[256,1152]{1,0:T(8,128)(2,1)S(1)} %get-tuple-element.45.first2.left2, ...), custom_call_target="tpu_custom_call", output_to_operand_aliasing={{0}: (5, {}), {1}: (6, {})} | custom-call | tf_op jit(solution)/shard_map/pallas_call | solution.py:218
  40.3 3.2 %shard_map.63 = (f32[512,1152]{1,0:T(8,128)S(1)}, f32[512,1152]{1,0:T(8,128)S(1)}) custom-call(f32[2]{0:T(128)S(1)} %pad_maximum_fusion.scalars, bf16[256,1152]{1,0:T(8,128)(2,1)S(1)} %get-tuple-element.46.first1.left1, bf16[256,1152]{1,0:T(8,128)(2,1)S(1)} %get-tuple-element.45.first2.left2, ...), custom_call_target="tpu_custom_call", output_to_operand_aliasing={{0}: (5, {}), {1}: (6, {})} | custom-call | tf_op jit(solution)/shard_map/pallas_call | solution.py:218
  43.5 0.0 collective-permute-done.right1
  43.5 0.0 collective-permute-done.1.right2
  43.5 0.1 collective-permute-start.9
  43.6 4.1 %collective-permute-start.5 = (bf16[256,1152]{1,0:T(8,128)(2,1)S(1)}, bf16[256,1152]{1,0:T(8,128)(2,1)S(1)}, u32[]{:S(2)}, u32[]{:S(2)}) collective-permute-start(bf16[256,1152]{1,0:T(8,128)(2,1)S(1)} %collective-permute-done.right1), channel_id=1, source_target_pairs={{0,63},{1,2},{2,1},{3,4},{4,3},{5,6},{6,5},{7,8},{8,7},{9,10},{10,... | collective-permute-start | bytes 1769480 | tf_op jit(solution)/shard_map/ppermute | solution.py:212
  47.7 3.2 %shard_map.64 = (f32[512,1152]{1,0:T(8,128)S(1)}, f32[512,1152]{1,0:T(8,128)S(1)}) custom-call(f32[2]{0:T(128)S(1)} %pad_maximum_fusion.scalars, bf16[256,1152]{1,0:T(8,128)(2,1)S(1)} %get-tuple-element.46.first1.left1, bf16[256,1152]{1,0:T(8,128)(2,1)S(1)} %get-tuple-element.45.first2.left2, ...), custom_call_target="tpu_custom_call", output_to_operand_aliasing={{0}: (5, {}), {1}: (6, {})} | custom-call | tf_op jit(solution)/shard_map/pallas_call | solution.py:218
  51.0 0.0 collective-permute-done.6.right1
  51.0 2.5 %collective-permute-done.7.right2 = bf16[256,1152]{1,0:T(8,128)(2,1)S(1)} collective-permute-done((bf16[256,1152]{1,0:T(8,128)(2,1)S(1)}, bf16[256,1152]{1,0:T(8,128)(2,1)S(1)}, u32[]{:S(2)}, u32[]{:S(2)}) %collective-permute-start.7) | collective-permute-done | bytes 589856 | tf_op jit(solution)/shard_map/ppermute | solution.py:212
  53.5 3.2 %shard_map.65 = (f32[512,1152]{1,0:T(8,128)S(1)}, f32[512,1152]{1,0:T(8,128)S(1)}) custom-call(f32[2]{0:T(128)S(1)} %pad_maximum_fusion.scalars, bf16[256,1152]{1,0:T(8,128)(2,1)S(1)} %get-tuple-element.46.first1.left1, bf16[256,1152]{1,0:T(8,128)(2,1)S(1)} %get-tuple-element.45.first2.left2, ...), custom_call_target="tpu_custom_call", output_to_operand_aliasing={{0}: (5, {}), {1}: (6, {})} | custom-call | tf_op jit(solution)/shard_map/pallas_call | solution.py:218
  56.7 0.0 collective-permute-done.8.both
  56.7 3.2 %shard_map.66 = (f32[512,1152]{1,0:T(8,128)S(1)}, f32[512,1152]{1,0:T(8,128)S(1)}) custom-call(f32[2]{0:T(128)S(1)} %pad_maximum_fusion.scalars, bf16[256,1152]{1,0:T(8,128)(2,1)S(1)} %get-tuple-element.46.first1.left1, bf16[256,1152]{1,0:T(8,128)(2,1)S(1)} %get-tuple-element.45.first2.left2, ...), custom_call_target="tpu_custom_call", output_to_operand_aliasing={{0}: (5, {}), {1}: (6, {})} | custom-call | tf_op jit(solution)/shard_map/pallas_call | solution.py:218
  59.9 0.0 collective-permute-done.9.right
  59.9 2.8 %shard_map.67 = (bf16[512,1152]{1,0:T(8,128)(2,1)}, bf16[512,1152]{1,0:T(8,128)(2,1)}) custom-call(f32[2]{0:T(128)S(1)} %pad_maximum_fusion.scalars, s32[1]{0:T(128)} %bitcast.even, bf16[256,1152]{1,0:T(8,128)(2,1)S(1)} %get-tuple-element.46.first1.left1, bf16[256,1152]{1,0:T(8,128)(2,1)S(1)} %get-tuple-element.45.first2.left2, ...), custom_call_target="tpu_custom_call" | custom-call | tf_op jit(solution)/shard_map/pallas_call | solution.py:243
  62.7 3.4 %collective-permute-done.5.right = bf16[256,1152]{1,0:T(8,128)(2,1)S(1)} collective-permute-done((bf16[256,1152]{1,0:T(8,128)(2,1)S(1)}, bf16[256,1152]{1,0:T(8,128)(2,1)S(1)}, u32[]{:S(2)}, u32[]{:S(2)}) %collective-permute-start.5) | collective-permute-done | bytes 589856 | tf_op jit(solution)/shard_map/ppermute | solution.py:212
  66.1 2.8 %shard_map.68 = (bf16[512,1152]{1,0:T(8,128)(2,1)}, bf16[512,1152]{1,0:T(8,128)(2,1)}) custom-call(f32[2]{0:T(128)S(1)} %pad_maximum_fusion.scalars, s32[1]{0:T(128)} %bitcast.even, bf16[256,1152]{1,0:T(8,128)(2,1)S(1)} %get-tuple-element.43.second1.left1, ...), custom_call_target="tpu_custom_call", output_to_operand_aliasing={{0}: (8, {}), {1}: (9, {})} | custom-call | tf_op jit(solution)/shard_map/pallas_call | solution.py:243
Async XLA Ops:
  2.2 27.3 %collective-permute-start.4 = (bf16[512,1152]{1,0:T(8,128)(2,1)S(1)}, bf16[512,1152]{1,0:T(8,128)(2,1)S(1)}, u32[]{:S(2)}, u32[]{:S(2)}) collective-permute-start(bf16[512,1152]{1,0:T(8,128)(2,1)S(1)} %get-tuple-element.60), channel_id=1, source_target_pairs={{0,64},{1,65},{2,66},{3,67},{4,68},{5,69},{6,70},{7,71},{8,72},{9,... | collective-permute-start | bytes 3538952 | tf_op jit(solution)/shard_map/ppermute | solution.py:212
  5.6 18.9 %collective-permute-start.2 = (bf16[256,1152]{1,0:T(8,128)(2,1)S(1)}, bf16[256,1152]{1,0:T(8,128)(2,1)S(1)}, u32[]{:S(2)}, u32[]{:S(2)}) collective-permute-start(bf16[256,1152]{1,0:T(8,128)(2,1)S(1)} %get-tuple-element.46.first1.left1), channel_id=1, source_target_pairs={{0,1},{1,0},{2,3},{3,2},{4,5},{5,4},{6,7},{7,6},{8,9},{9,8},{10,11... | collective-permute-start | bytes 1769480 | tf_op jit(solution)/shard_map/ppermute | solution.py:212
  5.6 22.6 %collective-permute-start.3 = (bf16[256,1152]{1,0:T(8,128)(2,1)S(1)}, bf16[256,1152]{1,0:T(8,128)(2,1)S(1)}, u32[]{:S(2)}, u32[]{:S(2)}) collective-permute-start(bf16[256,1152]{1,0:T(8,128)(2,1)S(1)} %get-tuple-element.43.second1.left1), channel_id=1, source_target_pairs={{0,63},{1,2},{2,1},{3,4},{4,3},{5,6},{6,5},{7,8},{8,7},{9,10},{10,... | collective-permute-start | bytes 1769480 | tf_op jit(solution)/shard_map/ppermute | solution.py:212
  16.4 27.1 %collective-permute-start = (bf16[256,1152]{1,0:T(8,128)(2,1)S(1)}, bf16[256,1152]{1,0:T(8,128)(2,1)S(1)}, u32[]{:S(2)}, u32[]{:S(2)}) collective-permute-start(bf16[256,1152]{1,0:T(8,128)(2,1)S(1)} %get-tuple-element.45.first2.left2), channel_id=1, source_target_pairs={{0,1},{1,0},{2,3},{3,2},{4,5},{5,4},{6,7},{7,6},{8,9},{9,8},{10,11... | collective-permute-start | bytes 1769480 | tf_op jit(solution)/shard_map/ppermute | solution.py:212
  16.5 27.0 %collective-permute-start.1 = (bf16[256,1152]{1,0:T(8,128)(2,1)S(1)}, bf16[256,1152]{1,0:T(8,128)(2,1)S(1)}, u32[]{:S(2)}, u32[]{:S(2)}) collective-permute-start(bf16[256,1152]{1,0:T(8,128)(2,1)S(1)} %get-tuple-element.44.second2.left2), channel_id=1, source_target_pairs={{0,63},{1,2},{2,1},{3,4},{4,3},{5,6},{6,5},{7,8},{8,7},{9,10},{10,... | collective-permute-start | bytes 1769480 | tf_op jit(solution)/shard_map/ppermute | solution.py:212
  28.2 28.5 %collective-permute-start.8 = (bf16[512,1152]{1,0:T(8,128)(2,1)S(1)}, bf16[512,1152]{1,0:T(8,128)(2,1)S(1)}, u32[]{:S(2)}, u32[]{:S(2)}) collective-permute-start(bf16[512,1152]{1,0:T(8,128)(2,1)S(1)} %get-tuple-element.75), channel_id=1, source_target_pairs={{0,64},{1,65},{2,66},{3,67},{4,68},{5,69},{6,70},{7,71},{8,72},{9,... | collective-permute-start | bytes 3538952 | tf_op jit(solution)/shard_map/ppermute | solution.py:212
  29.6 21.4 %collective-permute-start.6 = (bf16[256,1152]{1,0:T(8,128)(2,1)S(1)}, bf16[256,1152]{1,0:T(8,128)(2,1)S(1)}, u32[]{:S(2)}, u32[]{:S(2)}) collective-permute-start(bf16[256,1152]{1,0:T(8,128)(2,1)S(1)} %collective-permute-done.3.right2), channel_id=1, source_target_pairs={{0,1},{1,0},{2,3},{3,2},{4,5},{5,4},{6,7},{7,6},{8,9},{9,8},{10,11... | collective-permute-start | bytes 1769480 | tf_op jit(solution)/shard_map/ppermute | solution.py:212
  29.6 23.9 %collective-permute-start.7 = (bf16[256,1152]{1,0:T(8,128)(2,1)S(1)}, bf16[256,1152]{1,0:T(8,128)(2,1)S(1)}, u32[]{:S(2)}, u32[]{:S(2)}) collective-permute-start(bf16[256,1152]{1,0:T(8,128)(2,1)S(1)} %collective-permute-done.2.right1), channel_id=1, source_target_pairs={{0,63},{1,2},{2,1},{3,4},{4,3},{5,6},{6,5},{7,8},{8,7},{9,10},{10,... | collective-permute-start | bytes 1769480 | tf_op jit(solution)/shard_map/ppermute | solution.py:212
  43.5 16.4 %collective-permute-start.9 = (bf16[256,1152]{1,0:T(8,128)(2,1)S(1)}, bf16[256,1152]{1,0:T(8,128)(2,1)S(1)}, u32[]{:S(2)}, u32[]{:S(2)}) collective-permute-start(bf16[256,1152]{1,0:T(8,128)(2,1)S(1)} %collective-permute-done.1.right2), channel_id=1, source_target_pairs={{0,1},{1,0},{2,3},{3,2},{4,5},{5,4},{6,7},{7,6},{8,9},{9,8},{10,11... | collective-permute-start | bytes 1769480 | tf_op jit(solution)/shard_map/ppermute | solution.py:212
  43.6 22.5 %collective-permute-start.5 = (bf16[256,1152]{1,0:T(8,128)(2,1)S(1)}, bf16[256,1152]{1,0:T(8,128)(2,1)S(1)}, u32[]{:S(2)}, u32[]{:S(2)}) collective-permute-start(bf16[256,1152]{1,0:T(8,128)(2,1)S(1)} %collective-permute-done.right1), channel_id=1, source_target_pairs={{0,63},{1,2},{2,1},{3,4},{4,3},{5,6},{6,5},{7,8},{8,7},{9,10},{10,... | collective-permute-start | bytes 1769480 | tf_op jit(solution)/shard_map/ppermute | solution.py:212

commit v4 on v3

--- a/solution.py
+++ b/solution.py
@@ -48,38 +48,30 @@
     *outs, both, sems = refs
     blocks = (outs[:3], outs[3:])
     rows = blocks[0][0].shape[0]
-    tiles = rows // TILE
-
-    def fetch(slot, source, tile):
+
+    def fetch(slot, source):
         return pltpu.make_async_copy(
-            source.at[pl.ds(start + tile * TILE, TILE)],
-            blocks[slot][1].at[pl.ds(tile * TILE, TILE)],
-            sems.at[slot, tile],
+            source.at[pl.ds(start, rows)], blocks[slot][1], sems.at[slot]
         )
-
-    def begin(sources):
-        for tile in range(tiles):
-            for slot, source in enumerate(sources):
-                fetch(slot, source, tile).start()
 
     @pl.when(even[0] == 1)
     def _():
-        begin((texts, images))
+        fetch(0, texts).start()
+        fetch(1, images).start()
 
     @pl.when(even[0] != 1)
     def _():
-        begin((images, texts))
-
-    for tile in range(tiles):
-        at = pl.ds(tile * TILE, TILE)
-        for slot, (half, raw, norm) in enumerate(blocks):
-            fetch(slot, images, tile).wait()
-            values = raw[at].astype(jnp.float32)
-            inverse = lax.rsqrt(jnp.sum(values * values, axis=-1, keepdims=True) + 1e-06)
-            rounded = (values * inverse).astype(jnp.bfloat16)
-            half[at] = rounded
-            both[pl.ds(slot * rows + tile * TILE, TILE)] = rounded
-            norm[at] = jnp.broadcast_to(inverse, (TILE, 128))
+        fetch(0, images).start()
+        fetch(1, texts).start()
+
+    for slot, (half, raw, norm) in enumerate(blocks):
+        fetch(slot, images).wait()
+        values = raw[...].astype(jnp.float32)
+        inverse = lax.rsqrt(jnp.sum(values * values, axis=-1, keepdims=True) + 1e-06)
+        rounded = (values * inverse).astype(jnp.bfloat16)
+        half[...] = rounded
+        both[pl.ds(slot * rows, rows)] = rounded
+        norm[...] = jnp.broadcast_to(inverse, (rows, 128))
 
 
 def prepare(start, rows, even, images, texts):
@@ -92,7 +84,7 @@
         outs,
         [SMEM, HBM, HBM],
         [VMEM] * len(outs),
-        [pltpu.SemaphoreType.DMA((2, rows // TILE))],
+        [pltpu.SemaphoreType.DMA((2,))],
         limit=50,
     )(even, images, texts)
 

time: 69.3 us -> 69.2 us (level)
  no operation moved by 1% of the time
where the time goes in v4:
time: 69.2 us; the launch traced here: 69 us
  Pallas kernels  30.3 us (44%)
  starting transfers between devices  26.6 us (38%)
  waiting for transfers between devices  9.77 us (14%)
  between operations  2.22 us (3%)
    ppermute x10, starting transfers between devices, send(): return lax.ppermute(block, AXES, route)  26.6 us
    pallas_call x5, Pallas kernels, add(): call(body, totals, [SMEM] + [VMEM] * (6 + len(rights)), [VMEM] * 2, alias...  16 us
    ppermute x10, waiting for transfers between devices, send(): return lax.ppermute(block, AXES, route)  9.77 us
    pallas_call x1, Pallas kernels, on_device(): call(own_kernel, totals + units, [SMEM] + [VMEM] * 12, [VMEM] * 6)  5.69 us
    pallas_call x2, Pallas kernels, last(): call(body, [shape(rows, width, jnp.bfloat16)] * 2, [SMEM] * 2 + [VMEM] *...  5.62 us
    pallas_call x2, Pallas kernels, prepare(): call(functools.partial(prepare_kernel, start), outs, [SMEM, HBM, HBM], [V...  3 us
  transfers between devices with their start and end apart: 10, of which 3 were waited for; matrix products, arithmetic and copies ran while one was open for 0% of the time, Pallas kernels for 38%

profile of v4, /device:TPU:1, one launch (start us, length us, event | category | flops | bytes accessed | tf_op | source)
XLA Modules:
  0.0 69.0 jit_solution(15349777081150643693)
XLA Ops:
  0.6 1.5 %shard_map.59 = (bf16[256,1152]{1,0:T(8,128)(2,1)S(1)}, bf16[256,1152]{1,0:T(8,128)(2,1)S(1)}, f32[256,128]{1,0:T(8,128)S(1)}, bf16[256,1152]{1,0:T(8,128)(2,1)S...) custom-call(s32[1]{0:T(128)} %bitcast.even, bf16[512,1152]{1,0:T(8,128)(2,1)} %images.3, ...), custom_call_target="tpu_custom_call" | custom-call | tf_op jit(solution)/shard_map/pallas_call | solution.py:82
  2.2 3.3 %collective-permute-start.4 = (bf16[512,1152]{1,0:T(8,128)(2,1)S(1)}, bf16[512,1152]{1,0:T(8,128)(2,1)S(1)}, u32[]{:S(2)}, u32[]{:S(2)}) collective-permute-start(bf16[512,1152]{1,0:T(8,128)(2,1)S(1)} %get-tuple-element.60), channel_id=1, source_target_pairs={{0,64},{1,65},{2,66},{3,67},{4,68},{5,69},{6,70},{7,71},{8,72},{9,... | collective-permute-start | bytes 3538952 | tf_op jit(solution)/shard_map/ppermute | solution.py:204
  5.5 0.0 collective-permute-start.2
  5.5 9.2 %collective-permute-start.3 = (bf16[256,1152]{1,0:T(8,128)(2,1)S(1)}, bf16[256,1152]{1,0:T(8,128)(2,1)S(1)}, u32[]{:S(2)}, u32[]{:S(2)}) collective-permute-start(bf16[256,1152]{1,0:T(8,128)(2,1)S(1)} %get-tuple-element.43.second1.left1), channel_id=1, source_target_pairs={{0,63},{1,2},{2,1},{3,4},{4,3},{5,6},{6,5},{7,8},{8,7},{9,10},{10,... | collective-permute-start | bytes 1769480 | tf_op jit(solution)/shard_map/ppermute | solution.py:204
  14.7 1.5 %shard_map.60 = (bf16[256,1152]{1,0:T(8,128)(2,1)S(1)}, bf16[256,1152]{1,0:T(8,128)(2,1)S(1)}, f32[256,128]{1,0:T(8,128)S(1)}, bf16[256,1152]{1,0:T(8,128)(2,1)S...) custom-call(s32[1]{0:T(128)} %bitcast.even, bf16[512,1152]{1,0:T(8,128)(2,1)} %images.3, ...), custom_call_target="tpu_custom_call" | custom-call | tf_op jit(solution)/shard_map/pallas_call | solution.py:82
  16.2 0.1 collective-permute-start
  16.3 0.9 %collective-permute-start.1 = (bf16[256,1152]{1,0:T(8,128)(2,1)S(1)}, bf16[256,1152]{1,0:T(8,128)(2,1)S(1)}, u32[]{:S(2)}, u32[]{:S(2)}) collective-permute-start(bf16[256,1152]{1,0:T(8,128)(2,1)S(1)} %get-tuple-element.44.second2.left2), channel_id=1, source_target_pairs={{0,63},{1,2},{2,1},{3,4},{4,3},{5,6},{6,5},{7,8},{8,7},{9,10},{10,... | collective-permute-start | bytes 1769480 | tf_op jit(solution)/shard_map/ppermute | solution.py:204
  18.5 0.1 pad_maximum_fusion.scalars
  18.6 5.7 %shard_map.61 = (f32[512,1152]{1,0:T(8,128)S(1)}, f32[512,1152]{1,0:T(8,128)S(1)}, f32[512,1152]{1,0:T(8,128)S(1)}, f32[512,1152]{1,0:T(8,128)S(1)}, f32[512,128]{1,0:T(8,128)S(1)}, /*index=5*/f32[512,128]{1,0:T(8,128)S(1)}) custom-call(f32[2]{0:T(128)S(1)} %pad_maximum_fusion.scalars, bf16[256,1152]{1,0:T(8,128)(2,1)S(1)} %get-tuple-element.46.first1.left1, ...), custom_call_target="tpu_custom_call" | custom-call | tf_op jit(solution)/shard_map/pallas_call | solution.py:218
  24.3 0.0 collective-permute-done.2.right1
  24.3 3.8 %collective-permute-done.3.right2 = bf16[256,1152]{1,0:T(8,128)(2,1)S(1)} collective-permute-done((bf16[256,1152]{1,0:T(8,128)(2,1)S(1)}, bf16[256,1152]{1,0:T(8,128)(2,1)S(1)}, u32[]{:S(2)}, u32[]{:S(2)}) %collective-permute-start.3) | collective-permute-done | bytes 589856 | tf_op jit(solution)/shard_map/ppermute | solution.py:204
  28.1 1.3 %collective-permute-start.8 = (bf16[512,1152]{1,0:T(8,128)(2,1)S(1)}, bf16[512,1152]{1,0:T(8,128)(2,1)S(1)}, u32[]{:S(2)}, u32[]{:S(2)}) collective-permute-start(bf16[512,1152]{1,0:T(8,128)(2,1)S(1)} %get-tuple-element.75), channel_id=1, source_target_pairs={{0,64},{1,65},{2,66},{3,67},{4,68},{5,69},{6,70},{7,71},{8,72},{9,... | collective-permute-start | bytes 3538952 | tf_op jit(solution)/shard_map/ppermute | solution.py:204
  29.5 0.0 collective-permute-start.6
  29.5 0.0 collective-permute-done.4.both
  29.5 7.5 %collective-permute-start.7 = (bf16[256,1152]{1,0:T(8,128)(2,1)S(1)}, bf16[256,1152]{1,0:T(8,128)(2,1)S(1)}, u32[]{:S(2)}, u32[]{:S(2)}) collective-permute-start(bf16[256,1152]{1,0:T(8,128)(2,1)S(1)} %collective-permute-done.2.right1), channel_id=1, source_target_pairs={{0,63},{1,2},{2,1},{3,4},{4,3},{5,6},{6,5},{7,8},{8,7},{9,10},{10,... | collective-permute-start | bytes 1769480 | tf_op jit(solution)/shard_map/ppermute | solution.py:204
  37.0 3.2 %shard_map.62 = (f32[512,1152]{1,0:T(8,128)S(1)}, f32[512,1152]{1,0:T(8,128)S(1)}) custom-call(f32[2]{0:T(128)S(1)} %pad_maximum_fusion.scalars, bf16[256,1152]{1,0:T(8,128)(2,1)S(1)} %get-tuple-element.46.first1.left1, bf16[256,1152]{1,0:T(8,128)(2,1)S(1)} %get-tuple-element.45.first2.left2, ...), custom_call_target="tpu_custom_call", output_to_operand_aliasing={{0}: (5, {}), {1}: (6, {})} | custom-call | tf_op jit(solution)/shard_map/pallas_call | solution.py:210
  40.2 3.2 %shard_map.63 = (f32[512,1152]{1,0:T(8,128)S(1)}, f32[512,1152]{1,0:T(8,128)S(1)}) custom-call(f32[2]{0:T(128)S(1)} %pad_maximum_fusion.scalars, bf16[256,1152]{1,0:T(8,128)(2,1)S(1)} %get-tuple-element.46.first1.left1, bf16[256,1152]{1,0:T(8,128)(2,1)S(1)} %get-tuple-element.45.first2.left2, ...), custom_call_target="tpu_custom_call", output_to_operand_aliasing={{0}: (5, {}), {1}: (6, {})} | custom-call | tf_op jit(solution)/shard_map/pallas_call | solution.py:210
  43.4 0.0 collective-permute-done.right1
  43.4 0.0 collective-permute-done.1.right2
  43.4 0.1 collective-permute-start.9
  43.5 4.1 %collective-permute-start.5 = (bf16[256,1152]{1,0:T(8,128)(2,1)S(1)}, bf16[256,1152]{1,0:T(8,128)(2,1)S(1)}, u32[]{:S(2)}, u32[]{:S(2)}) collective-permute-start(bf16[256,1152]{1,0:T(8,128)(2,1)S(1)} %collective-permute-done.right1), channel_id=1, source_target_pairs={{0,63},{1,2},{2,1},{3,4},{4,3},{5,6},{6,5},{7,8},{8,7},{9,10},{10,... | collective-permute-start | bytes 1769480 | tf_op jit(solution)/shard_map/ppermute | solution.py:204
  47.6 3.2 %shard_map.64 = (f32[512,1152]{1,0:T(8,128)S(1)}, f32[512,1152]{1,0:T(8,128)S(1)}) custom-call(f32[2]{0:T(128)S(1)} %pad_maximum_fusion.scalars, bf16[256,1152]{1,0:T(8,128)(2,1)S(1)} %get-tuple-element.46.first1.left1, bf16[256,1152]{1,0:T(8,128)(2,1)S(1)} %get-tuple-element.45.first2.left2, ...), custom_call_target="tpu_custom_call", output_to_operand_aliasing={{0}: (5, {}), {1}: (6, {})} | custom-call | tf_op jit(solution)/shard_map/pallas_call | solution.py:210
  50.9 0.0 collective-permute-done.6.right1
  50.9 2.5 %collective-permute-done.7.right2 = bf16[256,1152]{1,0:T(8,128)(2,1)S(1)} collective-permute-done((bf16[256,1152]{1,0:T(8,128)(2,1)S(1)}, bf16[256,1152]{1,0:T(8,128)(2,1)S(1)}, u32[]{:S(2)}, u32[]{:S(2)}) %collective-permute-start.7) | collective-permute-done | bytes 589856 | tf_op jit(solution)/shard_map/ppermute | solution.py:204
  53.4 3.2 %shard_map.65 = (f32[512,1152]{1,0:T(8,128)S(1)}, f32[512,1152]{1,0:T(8,128)S(1)}) custom-call(f32[2]{0:T(128)S(1)} %pad_maximum_fusion.scalars, bf16[256,1152]{1,0:T(8,128)(2,1)S(1)} %get-tuple-element.46.first1.left1, bf16[256,1152]{1,0:T(8,128)(2,1)S(1)} %get-tuple-element.45.first2.left2, ...), custom_call_target="tpu_custom_call", output_to_operand_aliasing={{0}: (5, {}), {1}: (6, {})} | custom-call | tf_op jit(solution)/shard_map/pallas_call | solution.py:210
  56.6 0.0 collective-permute-done.8.both
  56.6 3.2 %shard_map.66 = (f32[512,1152]{1,0:T(8,128)S(1)}, f32[512,1152]{1,0:T(8,128)S(1)}) custom-call(f32[2]{0:T(128)S(1)} %pad_maximum_fusion.scalars, bf16[256,1152]{1,0:T(8,128)(2,1)S(1)} %get-tuple-element.46.first1.left1, bf16[256,1152]{1,0:T(8,128)(2,1)S(1)} %get-tuple-element.45.first2.left2, ...), custom_call_target="tpu_custom_call", output_to_operand_aliasing={{0}: (5, {}), {1}: (6, {})} | custom-call | tf_op jit(solution)/shard_map/pallas_call | solution.py:210
  59.8 0.0 collective-permute-done.9.right
  59.8 2.8 %shard_map.67 = (bf16[512,1152]{1,0:T(8,128)(2,1)}, bf16[512,1152]{1,0:T(8,128)(2,1)}) custom-call(f32[2]{0:T(128)S(1)} %pad_maximum_fusion.scalars, s32[1]{0:T(128)} %bitcast.even, bf16[256,1152]{1,0:T(8,128)(2,1)S(1)} %get-tuple-element.46.first1.left1, bf16[256,1152]{1,0:T(8,128)(2,1)S(1)} %get-tuple-element.45.first2.left2, ...), custom_call_target="tpu_custom_call" | custom-call | tf_op jit(solution)/shard_map/pallas_call | solution.py:235
  62.6 3.4 %collective-permute-done.5.right = bf16[256,1152]{1,0:T(8,128)(2,1)S(1)} collective-permute-done((bf16[256,1152]{1,0:T(8,128)(2,1)S(1)}, bf16[256,1152]{1,0:T(8,128)(2,1)S(1)}, u32[]{:S(2)}, u32[]{:S(2)}) %collective-permute-start.5) | collective-permute-done | bytes 589856 | tf_op jit(solution)/shard_map/ppermute | solution.py:204
  66.0 2.8 %shard_map.68 = (bf16[512,1152]{1,0:T(8,128)(2,1)}, bf16[512,1152]{1,0:T(8,128)(2,1)}) custom-call(f32[2]{0:T(128)S(1)} %pad_maximum_fusion.scalars, s32[1]{0:T(128)} %bitcast.even, bf16[256,1152]{1,0:T(8,128)(2,1)S(1)} %get-tuple-element.43.second1.left1, ...), custom_call_target="tpu_custom_call", output_to_operand_aliasing={{0}: (8, {}), {1}: (9, {})} | custom-call | tf_op jit(solution)/shard_map/pallas_call | solution.py:235
Async XLA Ops:
  2.2 27.3 %collective-permute-start.4 = (bf16[512,1152]{1,0:T(8,128)(2,1)S(1)}, bf16[512,1152]{1,0:T(8,128)(2,1)S(1)}, u32[]{:S(2)}, u32[]{:S(2)}) collective-permute-start(bf16[512,1152]{1,0:T(8,128)(2,1)S(1)} %get-tuple-element.60), channel_id=1, source_target_pairs={{0,64},{1,65},{2,66},{3,67},{4,68},{5,69},{6,70},{7,71},{8,72},{9,... | collective-permute-start | bytes 3538952 | tf_op jit(solution)/shard_map/ppermute | solution.py:204
  5.5 18.8 %collective-permute-start.2 = (bf16[256,1152]{1,0:T(8,128)(2,1)S(1)}, bf16[256,1152]{1,0:T(8,128)(2,1)S(1)}, u32[]{:S(2)}, u32[]{:S(2)}) collective-permute-start(bf16[256,1152]{1,0:T(8,128)(2,1)S(1)} %get-tuple-element.46.first1.left1), channel_id=1, source_target_pairs={{0,1},{1,0},{2,3},{3,2},{4,5},{5,4},{6,7},{7,6},{8,9},{9,8},{10,11... | collective-permute-start | bytes 1769480 | tf_op jit(solution)/shard_map/ppermute | solution.py:204
  5.5 22.6 %collective-permute-start.3 = (bf16[256,1152]{1,0:T(8,128)(2,1)S(1)}, bf16[256,1152]{1,0:T(8,128)(2,1)S(1)}, u32[]{:S(2)}, u32[]{:S(2)}) collective-permute-start(bf16[256,1152]{1,0:T(8,128)(2,1)S(1)} %get-tuple-element.43.second1.left1), channel_id=1, source_target_pairs={{0,63},{1,2},{2,1},{3,4},{4,3},{5,6},{6,5},{7,8},{8,7},{9,10},{10,... | collective-permute-start | bytes 1769480 | tf_op jit(solution)/shard_map/ppermute | solution.py:204
  16.2 27.2 %collective-permute-start = (bf16[256,1152]{1,0:T(8,128)(2,1)S(1)}, bf16[256,1152]{1,0:T(8,128)(2,1)S(1)}, u32[]{:S(2)}, u32[]{:S(2)}) collective-permute-start(bf16[256,1152]{1,0:T(8,128)(2,1)S(1)} %get-tuple-element.45.first2.left2), channel_id=1, source_target_pairs={{0,1},{1,0},{2,3},{3,2},{4,5},{5,4},{6,7},{7,6},{8,9},{9,8},{10,11... | collective-permute-start | bytes 1769480 | tf_op jit(solution)/shard_map/ppermute | solution.py:204
  16.3 27.1 %collective-permute-start.1 = (bf16[256,1152]{1,0:T(8,128)(2,1)S(1)}, bf16[256,1152]{1,0:T(8,128)(2,1)S(1)}, u32[]{:S(2)}, u32[]{:S(2)}) collective-permute-start(bf16[256,1152]{1,0:T(8,128)(2,1)S(1)} %get-tuple-element.44.second2.left2), channel_id=1, source_target_pairs={{0,63},{1,2},{2,1},{3,4},{4,3},{5,6},{6,5},{7,8},{8,7},{9,10},{10,... | collective-permute-start | bytes 1769480 | tf_op jit(solution)/shard_map/ppermute | solution.py:204
  28.1 28.5 %collective-permute-start.8 = (bf16[512,1152]{1,0:T(8,128)(2,1)S(1)}, bf16[512,1152]{1,0:T(8,128)(2,1)S(1)}, u32[]{:S(2)}, u32[]{:S(2)}) collective-permute-start(bf16[512,1152]{1,0:T(8,128)(2,1)S(1)} %get-tuple-element.75), channel_id=1, source_target_pairs={{0,64},{1,65},{2,66},{3,67},{4,68},{5,69},{6,70},{7,71},{8,72},{9,... | collective-permute-start | bytes 3538952 | tf_op jit(solution)/shard_map/ppermute | solution.py:204
  29.5 21.4 %collective-permute-start.6 = (bf16[256,1152]{1,0:T(8,128)(2,1)S(1)}, bf16[256,1152]{1,0:T(8,128)(2,1)S(1)}, u32[]{:S(2)}, u32[]{:S(2)}) collective-permute-start(bf16[256,1152]{1,0:T(8,128)(2,1)S(1)} %collective-permute-done.3.right2), channel_id=1, source_target_pairs={{0,1},{1,0},{2,3},{3,2},{4,5},{5,4},{6,7},{7,6},{8,9},{9,8},{10,11... | collective-permute-start | bytes 1769480 | tf_op jit(solution)/shard_map/ppermute | solution.py:204
  29.5 23.9 %collective-permute-start.7 = (bf16[256,1152]{1,0:T(8,128)(2,1)S(1)}, bf16[256,1152]{1,0:T(8,128)(2,1)S(1)}, u32[]{:S(2)}, u32[]{:S(2)}) collective-permute-start(bf16[256,1152]{1,0:T(8,128)(2,1)S(1)} %collective-permute-done.2.right1), channel_id=1, source_target_pairs={{0,63},{1,2},{2,1},{3,4},{4,3},{5,6},{6,5},{7,8},{8,7},{9,10},{10,... | collective-permute-start | bytes 1769480 | tf_op jit(solution)/shard_map/ppermute | solution.py:204
  43.4 16.4 %collective-permute-start.9 = (bf16[256,1152]{1,0:T(8,128)(2,1)S(1)}, bf16[256,1152]{1,0:T(8,128)(2,1)S(1)}, u32[]{:S(2)}, u32[]{:S(2)}) collective-permute-start(bf16[256,1152]{1,0:T(8,128)(2,1)S(1)} %collective-permute-done.1.right2), channel_id=1, source_target_pairs={{0,1},{1,0},{2,3},{3,2},{4,5},{5,4},{6,7},{7,6},{8,9},{9,8},{10,11... | collective-permute-start | bytes 1769480 | tf_op jit(solution)/shard_map/ppermute | solution.py:204
  43.5 22.5 %collective-permute-start.5 = (bf16[256,1152]{1,0:T(8,128)(2,1)S(1)}, bf16[256,1152]{1,0:T(8,128)(2,1)S(1)}, u32[]{:S(2)}, u32[]{:S(2)}) collective-permute-start(bf16[256,1152]{1,0:T(8,128)(2,1)S(1)} %collective-permute-done.right1), channel_id=1, source_target_pairs={{0,63},{1,2},{2,1},{3,4},{4,3},{5,6},{6,5},{7,8},{8,7},{9,10},{10,... | collective-permute-start | bytes 1769480 | tf_op jit(solution)/shard_map/ppermute | solution.py:204

commit v5 on v4

--- a/solution.py
+++ b/solution.py
@@ -163,10 +163,17 @@
 
     coefs = [coefficients(scale, bias, left[...], right[...]) for left in (left1, left2)]
     tiles = 2 * rows // TILE
+
+    def term(tile):
+        i, inner = divmod(tile * TILE, rows)
+        return product(coefs[i][inner : inner + TILE], right[...])
+
+    ahead = term(0)
     for tile in range(tiles):
-        i, inner = divmod(tile * TILE, rows)
         at = pl.ds(tile * TILE, TILE)
-        whole = given[at] + product(coefs[i][inner : inner + TILE], right[...])
+        whole = given[at] + ahead
+        if tile < tiles - 1:
+            ahead = term(tile + 1)
         along = jnp.sum(unit[at] * whole, axis=-1, keepdims=True)
         out[at] = ((whole - unit[at] * along) * norm[at][:, :1]).astype(jnp.bfloat16)
 

time: 69.2 us -> 69.2 us (level)
  no operation moved by 1% of the time
where the time goes in v5:
time: 69.2 us; the launch traced here: 69 us
  Pallas kernels  30.3 us (44%)
  starting transfers between devices  26.6 us (38%)
  waiting for transfers between devices  9.78 us (14%)
  between operations  2.22 us (3%)
    ppermute x10, starting transfers between devices, send(): return lax.ppermute(block, AXES, route)  26.6 us
    pallas_call x5, Pallas kernels, add(): call(body, totals, [SMEM] + [VMEM] * (6 + len(rights)), [VMEM] * 2, alias...  16 us
    ppermute x10, waiting for transfers between devices, send(): return lax.ppermute(block, AXES, route)  9.78 us
    pallas_call x1, Pallas kernels, on_device(): call(own_kernel, totals + units, [SMEM] + [VMEM] * 12, [VMEM] * 6)  5.69 us
    pallas_call x2, Pallas kernels, last(): call(body, [shape(rows, width, jnp.bfloat16)] * 2, [SMEM] * 2 + [VMEM] *...  5.62 us
    pallas_call x2, Pallas kernels, prepare(): call(functools.partial(prepare_kernel, start), outs, [SMEM, HBM, HBM], [V...  3 us
  transfers between devices with their start and end apart: 10, of which 3 were waited for; matrix products, arithmetic and copies ran while one was open for 0% of the time, Pallas kernels for 38%

profile of v5, /device:TPU:1, one launch (start us, length us, event | category | flops | bytes accessed | tf_op | source)
XLA Modules:
  0.0 69.0 jit_solution(8755537758840020558)
XLA Ops:
  0.6 1.5 %shard_map.59 = (bf16[256,1152]{1,0:T(8,128)(2,1)S(1)}, bf16[256,1152]{1,0:T(8,128)(2,1)S(1)}, f32[256,128]{1,0:T(8,128)S(1)}, bf16[256,1152]{1,0:T(8,128)(2,1)S...) custom-call(s32[1]{0:T(128)} %bitcast.even, bf16[512,1152]{1,0:T(8,128)(2,1)} %images.3, ...), custom_call_target="tpu_custom_call" | custom-call | tf_op jit(solution)/shard_map/pallas_call | solution.py:82
  2.2 3.3 %collective-permute-start.4 = (bf16[512,1152]{1,0:T(8,128)(2,1)S(1)}, bf16[512,1152]{1,0:T(8,128)(2,1)S(1)}, u32[]{:S(2)}, u32[]{:S(2)}) collective-permute-start(bf16[512,1152]{1,0:T(8,128)(2,1)S(1)} %get-tuple-element.60), channel_id=1, source_target_pairs={{0,64},{1,65},{2,66},{3,67},{4,68},{5,69},{6,70},{7,71},{8,72},{9,... | collective-permute-start | bytes 3538952 | tf_op jit(solution)/shard_map/ppermute | solution.py:211
  5.5 0.0 collective-permute-start.2
  5.5 9.2 %collective-permute-start.3 = (bf16[256,1152]{1,0:T(8,128)(2,1)S(1)}, bf16[256,1152]{1,0:T(8,128)(2,1)S(1)}, u32[]{:S(2)}, u32[]{:S(2)}) collective-permute-start(bf16[256,1152]{1,0:T(8,128)(2,1)S(1)} %get-tuple-element.43.second1.left1), channel_id=1, source_target_pairs={{0,63},{1,2},{2,1},{3,4},{4,3},{5,6},{6,5},{7,8},{8,7},{9,10},{10,... | collective-permute-start | bytes 1769480 | tf_op jit(solution)/shard_map/ppermute | solution.py:211
  14.7 1.5 %shard_map.60 = (bf16[256,1152]{1,0:T(8,128)(2,1)S(1)}, bf16[256,1152]{1,0:T(8,128)(2,1)S(1)}, f32[256,128]{1,0:T(8,128)S(1)}, bf16[256,1152]{1,0:T(8,128)(2,1)S...) custom-call(s32[1]{0:T(128)} %bitcast.even, bf16[512,1152]{1,0:T(8,128)(2,1)} %images.3, ...), custom_call_target="tpu_custom_call" | custom-call | tf_op jit(solution)/shard_map/pallas_call | solution.py:82
  16.2 0.1 collective-permute-start
  16.3 0.9 %collective-permute-start.1 = (bf16[256,1152]{1,0:T(8,128)(2,1)S(1)}, bf16[256,1152]{1,0:T(8,128)(2,1)S(1)}, u32[]{:S(2)}, u32[]{:S(2)}) collective-permute-start(bf16[256,1152]{1,0:T(8,128)(2,1)S(1)} %get-tuple-element.44.second2.left2), channel_id=1, source_target_pairs={{0,63},{1,2},{2,1},{3,4},{4,3},{5,6},{6,5},{7,8},{8,7},{9,10},{10,... | collective-permute-start | bytes 1769480 | tf_op jit(solution)/shard_map/ppermute | solution.py:211
  18.5 0.1 pad_maximum_fusion.scalars
  18.6 5.7 %shard_map.61 = (f32[512,1152]{1,0:T(8,128)S(1)}, f32[512,1152]{1,0:T(8,128)S(1)}, f32[512,1152]{1,0:T(8,128)S(1)}, f32[512,1152]{1,0:T(8,128)S(1)}, f32[512,128]{1,0:T(8,128)S(1)}, /*index=5*/f32[512,128]{1,0:T(8,128)S(1)}) custom-call(f32[2]{0:T(128)S(1)} %pad_maximum_fusion.scalars, bf16[256,1152]{1,0:T(8,128)(2,1)S(1)} %get-tuple-element.46.first1.left1, ...), custom_call_target="tpu_custom_call" | custom-call | tf_op jit(solution)/shard_map/pallas_call | solution.py:225
  24.3 0.0 collective-permute-done.2.right1
  24.3 3.8 %collective-permute-done.3.right2 = bf16[256,1152]{1,0:T(8,128)(2,1)S(1)} collective-permute-done((bf16[256,1152]{1,0:T(8,128)(2,1)S(1)}, bf16[256,1152]{1,0:T(8,128)(2,1)S(1)}, u32[]{:S(2)}, u32[]{:S(2)}) %collective-permute-start.3) | collective-permute-done | bytes 589856 | tf_op jit(solution)/shard_map/ppermute | solution.py:211
  28.1 1.3 %collective-permute-start.8 = (bf16[512,1152]{1,0:T(8,128)(2,1)S(1)}, bf16[512,1152]{1,0:T(8,128)(2,1)S(1)}, u32[]{:S(2)}, u32[]{:S(2)}) collective-permute-start(bf16[512,1152]{1,0:T(8,128)(2,1)S(1)} %get-tuple-element.75), channel_id=1, source_target_pairs={{0,64},{1,65},{2,66},{3,67},{4,68},{5,69},{6,70},{7,71},{8,72},{9,... | collective-permute-start | bytes 3538952 | tf_op jit(solution)/shard_map/ppermute | solution.py:211
  29.5 0.0 collective-permute-start.6
  29.5 0.0 collective-permute-done.4.both
  29.5 7.5 %collective-permute-start.7 = (bf16[256,1152]{1,0:T(8,128)(2,1)S(1)}, bf16[256,1152]{1,0:T(8,128)(2,1)S(1)}, u32[]{:S(2)}, u32[]{:S(2)}) collective-permute-start(bf16[256,1152]{1,0:T(8,128)(2,1)S(1)} %collective-permute-done.2.right1), channel_id=1, source_target_pairs={{0,63},{1,2},{2,1},{3,4},{4,3},{5,6},{6,5},{7,8},{8,7},{9,10},{10,... | collective-permute-start | bytes 1769480 | tf_op jit(solution)/shard_map/ppermute | solution.py:211
  37.0 3.2 %shard_map.62 = (f32[512,1152]{1,0:T(8,128)S(1)}, f32[512,1152]{1,0:T(8,128)S(1)}) custom-call(f32[2]{0:T(128)S(1)} %pad_maximum_fusion.scalars, bf16[256,1152]{1,0:T(8,128)(2,1)S(1)} %get-tuple-element.46.first1.left1, bf16[256,1152]{1,0:T(8,128)(2,1)S(1)} %get-tuple-element.45.first2.left2, ...), custom_call_target="tpu_custom_call", output_to_operand_aliasing={{0}: (5, {}), {1}: (6, {})} | custom-call | tf_op jit(solution)/shard_map/pallas_call | solution.py:217
  40.2 3.2 %shard_map.63 = (f32[512,1152]{1,0:T(8,128)S(1)}, f32[512,1152]{1,0:T(8,128)S(1)}) custom-call(f32[2]{0:T(128)S(1)} %pad_maximum_fusion.scalars, bf16[256,1152]{1,0:T(8,128)(2,1)S(1)} %get-tuple-element.46.first1.left1, bf16[256,1152]{1,0:T(8,128)(2,1)S(1)} %get-tuple-element.45.first2.left2, ...), custom_call_target="tpu_custom_call", output_to_operand_aliasing={{0}: (5, {}), {1}: (6, {})} | custom-call | tf_op jit(solution)/shard_map/pallas_call | solution.py:217
  43.4 0.0 collective-permute-done.right1
  43.4 0.0 collective-permute-done.1.right2
  43.4 0.1 collective-permute-start.9
  43.5 4.1 %collective-permute-start.5 = (bf16[256,1152]{1,0:T(8,128)(2,1)S(1)}, bf16[256,1152]{1,0:T(8,128)(2,1)S(1)}, u32[]{:S(2)}, u32[]{:S(2)}) collective-permute-start(bf16[256,1152]{1,0:T(8,128)(2,1)S(1)} %collective-permute-done.right1), channel_id=1, source_target_pairs={{0,63},{1,2},{2,1},{3,4},{4,3},{5,6},{6,5},{7,8},{8,7},{9,10},{10,... | collective-permute-start | bytes 1769480 | tf_op jit(solution)/shard_map/ppermute | solution.py:211
  47.6 3.2 %shard_map.64 = (f32[512,1152]{1,0:T(8,128)S(1)}, f32[512,1152]{1,0:T(8,128)S(1)}) custom-call(f32[2]{0:T(128)S(1)} %pad_maximum_fusion.scalars, bf16[256,1152]{1,0:T(8,128)(2,1)S(1)} %get-tuple-element.46.first1.left1, bf16[256,1152]{1,0:T(8,128)(2,1)S(1)} %get-tuple-element.45.first2.left2, ...), custom_call_target="tpu_custom_call", output_to_operand_aliasing={{0}: (5, {}), {1}: (6, {})} | custom-call | tf_op jit(solution)/shard_map/pallas_call | solution.py:217
  50.9 0.0 collective-permute-done.6.right1
  50.9 2.5 %collective-permute-done.7.right2 = bf16[256,1152]{1,0:T(8,128)(2,1)S(1)} collective-permute-done((bf16[256,1152]{1,0:T(8,128)(2,1)S(1)}, bf16[256,1152]{1,0:T(8,128)(2,1)S(1)}, u32[]{:S(2)}, u32[]{:S(2)}) %collective-permute-start.7) | collective-permute-done | bytes 589856 | tf_op jit(solution)/shard_map/ppermute | solution.py:211
  53.4 3.2 %shard_map.65 = (f32[512,1152]{1,0:T(8,128)S(1)}, f32[512,1152]{1,0:T(8,128)S(1)}) custom-call(f32[2]{0:T(128)S(1)} %pad_maximum_fusion.scalars, bf16[256,1152]{1,0:T(8,128)(2,1)S(1)} %get-tuple-element.46.first1.left1, bf16[256,1152]{1,0:T(8,128)(2,1)S(1)} %get-tuple-element.45.first2.left2, ...), custom_call_target="tpu_custom_call", output_to_operand_aliasing={{0}: (5, {}), {1}: (6, {})} | custom-call | tf_op jit(solution)/shard_map/pallas_call | solution.py:217
  56.6 0.0 collective-permute-done.8.both
  56.6 3.2 %shard_map.66 = (f32[512,1152]{1,0:T(8,128)S(1)}, f32[512,1152]{1,0:T(8,128)S(1)}) custom-call(f32[2]{0:T(128)S(1)} %pad_maximum_fusion.scalars, bf16[256,1152]{1,0:T(8,128)(2,1)S(1)} %get-tuple-element.46.first1.left1, bf16[256,1152]{1,0:T(8,128)(2,1)S(1)} %get-tuple-element.45.first2.left2, ...), custom_call_target="tpu_custom_call", output_to_operand_aliasing={{0}: (5, {}), {1}: (6, {})} | custom-call | tf_op jit(solution)/shard_map/pallas_call | solution.py:217
  59.8 0.0 collective-permute-done.9.right
  59.8 2.8 %shard_map.67 = (bf16[512,1152]{1,0:T(8,128)(2,1)}, bf16[512,1152]{1,0:T(8,128)(2,1)}) custom-call(f32[2]{0:T(128)S(1)} %pad_maximum_fusion.scalars, s32[1]{0:T(128)} %bitcast.even, bf16[256,1152]{1,0:T(8,128)(2,1)S(1)} %get-tuple-element.46.first1.left1, bf16[256,1152]{1,0:T(8,128)(2,1)S(1)} %get-tuple-element.45.first2.left2, ...), custom_call_target="tpu_custom_call" | custom-call | tf_op jit(solution)/shard_map/pallas_call | solution.py:242
  62.6 3.4 %collective-permute-done.5.right = bf16[256,1152]{1,0:T(8,128)(2,1)S(1)} collective-permute-done((bf16[256,1152]{1,0:T(8,128)(2,1)S(1)}, bf16[256,1152]{1,0:T(8,128)(2,1)S(1)}, u32[]{:S(2)}, u32[]{:S(2)}) %collective-permute-start.5) | collective-permute-done | bytes 589856 | tf_op jit(solution)/shard_map/ppermute | solution.py:211
  66.0 2.8 %shard_map.68 = (bf16[512,1152]{1,0:T(8,128)(2,1)}, bf16[512,1152]{1,0:T(8,128)(2,1)}) custom-call(f32[2]{0:T(128)S(1)} %pad_maximum_fusion.scalars, s32[1]{0:T(128)} %bitcast.even, bf16[256,1152]{1,0:T(8,128)(2,1)S(1)} %get-tuple-element.43.second1.left1, ...), custom_call_target="tpu_custom_call", output_to_operand_aliasing={{0}: (8, {}), {1}: (9, {})} | custom-call | tf_op jit(solution)/shard_map/pallas_call | solution.py:242
Async XLA Ops:
  2.2 27.3 %collective-permute-start.4 = (bf16[512,1152]{1,0:T(8,128)(2,1)S(1)}, bf16[512,1152]{1,0:T(8,128)(2,1)S(1)}, u32[]{:S(2)}, u32[]{:S(2)}) collective-permute-start(bf16[512,1152]{1,0:T(8,128)(2,1)S(1)} %get-tuple-element.60), channel_id=1, source_target_pairs={{0,64},{1,65},{2,66},{3,67},{4,68},{5,69},{6,70},{7,71},{8,72},{9,... | collective-permute-start | bytes 3538952 | tf_op jit(solution)/shard_map/ppermute | solution.py:211
  5.5 18.8 %collective-permute-start.2 = (bf16[256,1152]{1,0:T(8,128)(2,1)S(1)}, bf16[256,1152]{1,0:T(8,128)(2,1)S(1)}, u32[]{:S(2)}, u32[]{:S(2)}) collective-permute-start(bf16[256,1152]{1,0:T(8,128)(2,1)S(1)} %get-tuple-element.46.first1.left1), channel_id=1, source_target_pairs={{0,1},{1,0},{2,3},{3,2},{4,5},{5,4},{6,7},{7,6},{8,9},{9,8},{10,11... | collective-permute-start | bytes 1769480 | tf_op jit(solution)/shard_map/ppermute | solution.py:211
  5.5 22.6 %collective-permute-start.3 = (bf16[256,1152]{1,0:T(8,128)(2,1)S(1)}, bf16[256,1152]{1,0:T(8,128)(2,1)S(1)}, u32[]{:S(2)}, u32[]{:S(2)}) collective-permute-start(bf16[256,1152]{1,0:T(8,128)(2,1)S(1)} %get-tuple-element.43.second1.left1), channel_id=1, source_target_pairs={{0,63},{1,2},{2,1},{3,4},{4,3},{5,6},{6,5},{7,8},{8,7},{9,10},{10,... | collective-permute-start | bytes 1769480 | tf_op jit(solution)/shard_map/ppermute | solution.py:211
  16.2 27.2 %collective-permute-start = (bf16[256,1152]{1,0:T(8,128)(2,1)S(1)}, bf16[256,1152]{1,0:T(8,128)(2,1)S(1)}, u32[]{:S(2)}, u32[]{:S(2)}) collective-permute-start(bf16[256,1152]{1,0:T(8,128)(2,1)S(1)} %get-tuple-element.45.first2.left2), channel_id=1, source_target_pairs={{0,1},{1,0},{2,3},{3,2},{4,5},{5,4},{6,7},{7,6},{8,9},{9,8},{10,11... | collective-permute-start | bytes 1769480 | tf_op jit(solution)/shard_map/ppermute | solution.py:211
  16.3 27.1 %collective-permute-start.1 = (bf16[256,1152]{1,0:T(8,128)(2,1)S(1)}, bf16[256,1152]{1,0:T(8,128)(2,1)S(1)}, u32[]{:S(2)}, u32[]{:S(2)}) collective-permute-start(bf16[256,1152]{1,0:T(8,128)(2,1)S(1)} %get-tuple-element.44.second2.left2), channel_id=1, source_target_pairs={{0,63},{1,2},{2,1},{3,4},{4,3},{5,6},{6,5},{7,8},{8,7},{9,10},{10,... | collective-permute-start | bytes 1769480 | tf_op jit(solution)/shard_map/ppermute | solution.py:211
  28.1 28.5 %collective-permute-start.8 = (bf16[512,1152]{1,0:T(8,128)(2,1)S(1)}, bf16[512,1152]{1,0:T(8,128)(2,1)S(1)}, u32[]{:S(2)}, u32[]{:S(2)}) collective-permute-start(bf16[512,1152]{1,0:T(8,128)(2,1)S(1)} %get-tuple-element.75), channel_id=1, source_target_pairs={{0,64},{1,65},{2,66},{3,67},{4,68},{5,69},{6,70},{7,71},{8,72},{9,... | collective-permute-start | bytes 3538952 | tf_op jit(solution)/shard_map/ppermute | solution.py:211
  29.5 21.4 %collective-permute-start.6 = (bf16[256,1152]{1,0:T(8,128)(2,1)S(1)}, bf16[256,1152]{1,0:T(8,128)(2,1)S(1)}, u32[]{:S(2)}, u32[]{:S(2)}) collective-permute-start(bf16[256,1152]{1,0:T(8,128)(2,1)S(1)} %collective-permute-done.3.right2), channel_id=1, source_target_pairs={{0,1},{1,0},{2,3},{3,2},{4,5},{5,4},{6,7},{7,6},{8,9},{9,8},{10,11... | collective-permute-start | bytes 1769480 | tf_op jit(solution)/shard_map/ppermute | solution.py:211
  29.5 23.9 %collective-permute-start.7 = (bf16[256,1152]{1,0:T(8,128)(2,1)S(1)}, bf16[256,1152]{1,0:T(8,128)(2,1)S(1)}, u32[]{:S(2)}, u32[]{:S(2)}) collective-permute-start(bf16[256,1152]{1,0:T(8,128)(2,1)S(1)} %collective-permute-done.2.right1), channel_id=1, source_target_pairs={{0,63},{1,2},{2,1},{3,4},{4,3},{5,6},{6,5},{7,8},{8,7},{9,10},{10,... | collective-permute-start | bytes 1769480 | tf_op jit(solution)/shard_map/ppermute | solution.py:211
  43.4 16.4 %collective-permute-start.9 = (bf16[256,1152]{1,0:T(8,128)(2,1)S(1)}, bf16[256,1152]{1,0:T(8,128)(2,1)S(1)}, u32[]{:S(2)}, u32[]{:S(2)}) collective-permute-start(bf16[256,1152]{1,0:T(8,128)(2,1)S(1)} %collective-permute-done.1.right2), channel_id=1, source_target_pairs={{0,1},{1,0},{2,3},{3,2},{4,5},{5,4},{6,7},{7,6},{8,9},{9,8},{10,11... | collective-permute-start | bytes 1769480 | tf_op jit(solution)/shard_map/ppermute | solution.py:211
  43.5 22.5 %collective-permute-start.5 = (bf16[256,1152]{1,0:T(8,128)(2,1)S(1)}, bf16[256,1152]{1,0:T(8,128)(2,1)S(1)}, u32[]{:S(2)}, u32[]{:S(2)}) collective-permute-start(bf16[256,1152]{1,0:T(8,128)(2,1)S(1)} %collective-permute-done.right1), channel_id=1, source_target_pairs={{0,63},{1,2},{2,1},{3,4},{4,3},{5,6},{6,5},{7,8},{8,7},{9,10},{10,... | collective-permute-start | bytes 1769480 | tf_op jit(solution)/shard_map/ppermute | solution.py:211
